TPU v7x, 256 devices: a whole 4x4x8 slice. The times are simulated.
256 devices in a mesh: seqhi: 8 (over x, core), seqlo: 32 (over y, z).
Axes of the slice: x: 4, y: 4, z: 8, core: 2. Of those that a mesh axis runs over, the one named last changes fastest.
Arguments:
- queries: float32 [32768, 768], P(('seqhi', 'seqlo')), may hold values from -6 to 6
- keys: float32 [32768, 768], P(('seqhi', 'seqlo')), may hold values from -6 to 6
- values: float32 [32768, 768], P(('seqhi', 'seqlo')), may hold values from -6 to 6
- cotangent: float32 [32768, 768], P(('seqhi', 'seqlo')), may hold values from -6 to 6
Outputs:
- attended: float32 [32768, 768], P(('seqhi', 'seqlo'))
- query_grad: float32 [32768, 768], P(('seqhi', 'seqlo'))
- key_grad: float32 [32768, 768], P(('seqhi', 'seqlo'))
- value_grad: float32 [32768, 768], P(('seqhi', 'seqlo'))
All inputs are finite; a program needn't handle non-finite values.
Results may differ from a plain program's by a relative error of at most 0.0003.
Values sent between devices are 32-bit elements; how exact they have to be, the bound alone decides.
A program may use at most 128 MiB of HBM per device.

v0:
```python
import math

import jax
import jax.numpy as jnp
from jax import lax
from jax.sharding import PartitionSpec as P

HEADS = 12
BLOCK = 128


LOG_TWO = math.log(2.0)
HIGHEST_PRECISION = lax.Precision.HIGHEST


def from_partner(value, axis, distance):
    return lax.ppermute(value, axis, [(i, i ^ 1 << distance) for i in range(lax.axis_size(axis))])


def halve_rows(matrix):
    paired = matrix.reshape(matrix.shape[0] // 2, 2, matrix.shape[1])
    return 0.5 * (paired[:, 0] + paired[:, 1])


def spread_rows(matrix, factor):
    row_count = matrix.shape[0]
    columns = matrix.shape[1]
    scaled = matrix[:, None, :] * (1.0 / factor)
    return jnp.broadcast_to(scaled, (row_count, factor, columns)).reshape(
        row_count * factor, columns
    )


def bit_of(device_index, bit_number):
    return device_index // 2**bit_number % 2 == 1


def split_half(matrix, upper_half):
    middle = matrix.shape[0] // 2
    kept_half = jnp.where(upper_half, matrix[middle:], matrix[:middle])
    sent_half = jnp.where(upper_half, matrix[:middle], matrix[middle:])
    return (kept_half, sent_half)


def level_sweep(partials, device_index):
    result = []
    for height in range(len(partials)):
        moved = from_partner(partials[height], ("seqhi", "seqlo"), height)
        for bit_number in range(height - 1, -1, -1):
            kept_half, sent_half = split_half(moved, bit_of(device_index, bit_number))
            moved = kept_half + from_partner(sent_half, ("seqhi", "seqlo"), bit_number)
        result.append(moved)
    return result


def on_device(queries, keys, values, cotangent):
    local_tokens = queries.shape[0]
    features = queries.shape[1]
    head_dim = features // HEADS
    blocks = local_tokens // BLOCK
    local_depth = blocks.bit_length() - 1
    device_count = lax.axis_size(("seqhi", "seqlo"))
    device_depth = device_count.bit_length() - 1
    device_index = lax.axis_index(("seqhi", "seqlo"))
    score_scale = 1.0 / math.sqrt(head_dim)
    paired_rows = jnp.concatenate([keys, values], axis=1)
    coarse = [paired_rows]
    set_list = [paired_rows.reshape(blocks, BLOCK, 2 * features)]
    offset_list = [0.0]
    current = coarse[local_depth]
    for height in range(device_depth):
        arrived = from_partner(current, ("seqhi", "seqlo"), height)
        set_list.append(arrived[None])
        offset_list.append((local_depth + height) * LOG_TWO)
        if height + 1 < device_depth:
            upper_half = bit_of(device_index, height)
            lower_part = jnp.where(upper_half, arrived, current)
            upper_part = jnp.where(upper_half, current, arrived)
            current = halve_rows(jnp.concatenate([lower_part, upper_part], axis=0))
    set_count = len(set_list)
    stacked = jnp.stack(set_list, axis=1).reshape(blocks, set_count, BLOCK, 2, HEADS, head_dim)
    key_part = stacked[:, :, :, 0]
    value_part = stacked[:, :, :, 1]
    offsets = jnp.array(offset_list, jnp.float32)
    query_heads = queries.reshape(blocks, BLOCK, HEADS, head_dim)
    grad_heads = cotangent.reshape(blocks, BLOCK, HEADS, head_dim)
    scores = (
        jnp.einsum("bqhd,bskhd->bhqsk", query_heads, key_part, precision=HIGHEST_PRECISION)
        * score_scale
    )
    scores = scores + offsets[None, None, None, :, None]
    highest = jnp.max(scores, axis=(3, 4), keepdims=True)
    exponent = jnp.exp(scores - highest)
    weights = exponent / jnp.sum(exponent, axis=(3, 4), keepdims=True)
    attended = jnp.einsum("bhqsk,bskhd->bqhd", weights, value_part, precision=HIGHEST_PRECISION)
    row_dot = jnp.transpose(jnp.sum(attended * grad_heads, axis=3), (0, 2, 1))[..., None, None]
    prob_grad = jnp.einsum("bqhd,bskhd->bhqsk", grad_heads, value_part, precision=HIGHEST_PRECISION)
    score_grad = weights * (prob_grad - row_dot)
    query_grad = (
        jnp.einsum("bhqsk,bskhd->bqhd", score_grad, key_part, precision=HIGHEST_PRECISION)
        * score_scale
    )
    key_grad = (
        jnp.einsum("bhqsk,bqhd->bskhd", score_grad, query_heads, precision=HIGHEST_PRECISION)
        * score_scale
    )
    value_grad = jnp.einsum("bhqsk,bqhd->bskhd", weights, grad_heads, precision=HIGHEST_PRECISION)
    pair_grad = jnp.concatenate(
        [
            key_grad.reshape(blocks, set_count, BLOCK, features),
            value_grad.reshape(blocks, set_count, BLOCK, features),
        ],
        axis=3,
    )
    token_grad = pair_grad[:, 0].reshape(local_tokens, 2 * features)
    remote_grads = [
        jnp.sum(pair_grad[:, 1 + local_depth + height], axis=0) for height in range(device_depth)
    ]
    held = level_sweep(remote_grads, device_index)
    for height in range(device_depth):
        token_grad = token_grad + spread_rows(held[height], 2 ** (local_depth + height))
    attended_rows = attended.reshape(local_tokens, features)
    query_rows = query_grad.reshape(local_tokens, features)
    return (attended_rows, query_rows, token_grad[:, :features], token_grad[:, features:])


def solution(mesh):
    return jax.shard_map(
        on_device,
        mesh=mesh,
        in_specs=(
            P(("seqhi", "seqlo"), None),
            P(("seqhi", "seqlo"), None),
            P(("seqhi", "seqlo"), None),
            P(("seqhi", "seqlo"), None),
        ),
        out_specs=(
            P(("seqhi", "seqlo"), None),
            P(("seqhi", "seqlo"), None),
            P(("seqhi", "seqlo"), None),
            P(("seqhi", "seqlo"), None),
        ),
        check_vma=False,
    )
```

profile of v0, /device:TPU:6, one launch (start us, length us, event | category | flops | bytes accessed | tf_op | source)
XLA Modules:
  0.0 475.4 jit_solution(6534797418809009477)
XLA Ops:
  4.7 17.5 %collective-permute-done = f32[128,1536]{1,0:T(8,128)S(1)} collective-permute-done((f32[128,1536]{1,0:T(8,128)S(1)}, f32[128,1536]{1,0:T(8,128)S(1)}, u32[]{:S(2)}, u32[]{:S(2)}) %collective-permute-start) | collective-permute-done | bytes 786464 | tf_op jit(solution)/shard_map/ppermute | solution.py:17
  28.6 33.7 %collective-permute-done.1 = f32[128,1536]{1,0:T(8,128)S(1)} collective-permute-done((f32[128,1536]{1,0:T(8,128)S(1)}, f32[128,1536]{1,0:T(8,128)S(1)}, u32[]{:S(2)}, u32[]{:S(2)}) %collective-permute-start.1) | collective-permute-done | bytes 786464 | tf_op jit(solution)/shard_map/ppermute | solution.py:17
  65.3 6.3 %collective-permute-start.2 = (f32[128,1536]{1,0:T(8,128)S(1)}, f32[128,1536]{1,0:T(8,128)S(1)}, u32[]{:S(2)}, u32[]{:S(2)}) collective-permute-start(f32[128,1536]{1,0:T(8,128)S(1)} %bitcast.214), channel_id=1, source_target_pairs={{0,4},{1,5},{2,6},{3,7},{4,0},{5,1},{6,2},{7,3},{8,12},{9,13},{10,... | collective-permute-start | bytes 2359304 | tf_op jit(solution)/shard_map/ppermute | solution.py:17
  71.6 34.4 %collective-permute-done.2 = f32[128,1536]{1,0:T(8,128)S(1)} collective-permute-done((f32[128,1536]{1,0:T(8,128)S(1)}, f32[128,1536]{1,0:T(8,128)S(1)}, u32[]{:S(2)}, u32[]{:S(2)}) %collective-permute-start.2) | collective-permute-done | bytes 786464 | tf_op jit(solution)/shard_map/ppermute | solution.py:17
  110.7 16.7 %collective-permute-done.3 = f32[128,1536]{1,0:T(8,128)S(1)} collective-permute-done((f32[128,1536]{1,0:T(8,128)S(1)}, f32[128,1536]{1,0:T(8,128)S(1)}, u32[]{:S(2)}, u32[]{:S(2)}) %collective-permute-start.3) | collective-permute-done | bytes 786464 | tf_op jit(solution)/shard_map/ppermute | solution.py:17
  133.8 15.7 %collective-permute-done.4 = f32[128,1536]{1,0:T(8,128)S(1)} collective-permute-done((f32[128,1536]{1,0:T(8,128)S(1)}, f32[128,1536]{1,0:T(8,128)S(1)}, u32[]{:S(2)}, u32[]{:S(2)}) %collective-permute-start.4) | collective-permute-done | bytes 786464 | tf_op jit(solution)/shard_map/ppermute | solution.py:17
  167.6 11.0 %collective-permute-done.6 = f32[128,1536]{1,0:T(8,128)S(1)} collective-permute-done((f32[128,1536]{1,0:T(8,128)}, f32[128,1536]{1,0:T(8,128)S(1)}, u32[]{:S(2)}, u32[]{:S(2)}) %collective-permute-start.6) | collective-permute-done | bytes 786464 | tf_op jit(solution)/shard_map/ppermute | solution.py:17
  193.7 9.8 %collective-permute-done.7 = f32[128,1536]{1,0:T(8,128)} collective-permute-done((f32[128,1536]{1,0:T(8,128)}, f32[128,1536]{1,0:T(8,128)}, u32[]{:S(2)}, u32[]{:S(2)}) %collective-permute-start.7) | collective-permute-done | bytes 786464 | tf_op jit(solution)/shard_map/ppermute | solution.py:17
  205.9 13.8 %bitcast_reduce_fusion = (f32[12,128]{1,0:T(8,128)S(1)}, f32[12,9,128,128]{3,2,1,0:T(8,128)S(1)}) fusion(f32[9]{0:T(128)S(1)} %copy-done.31, f32[128,12,64,1]{0,2,3,1:T(8,128)S(1)} %bitcast.199, f32[1,9,128,2,12,64]{2,5,1,4,3,0:T(8,128)} %constant_dynamic-update-slice_fusion.2), kind=kOutput, calls=%fused_computation.18 | convolution fusion | flops 1364261376 | bytes 11016228 | tf_op jit(solution)/shard_map/bqhd,bskhd->bhqsk/dot_general | solution.py:88
  221.1 6.9 %fusion.41 = (f32[128,12]{0,1:T(8,128)S(1)}, f32[12,64,128,1]{2,1,3,0:T(8,128)}) fusion(f32[1,128,12,64]{1,3,2,0:T(8,128)S(1)} %bitcast.216, f32[12,9,128,128]{3,2,1,0:T(8,128)S(1)} %get-tuple-element.49, f32[12,128]{1,0:T(8,128)S(1)} %fusion.2, f32[12,128]{1,0:T(8,128)S(1)} %get-tuple-element.48, f32[9]{0:T(128)S(1)} %copy-done.31, ...), kind=kOutput, calls=%fused_computation.88 | convolution fusion | flops 1366227456 | bytes 11426304 | tf_op jit(solution)/shard_map/bhqsk,bskhd->bqhd/dot_general | solution.py:95
  228.0 11.6 %convolution_bitcast_fusion = f32[1,9,128,12,64]{2,4,1,3,0:T(8,128)} fusion(f32[128,12,64,1]{0,2,3,1:T(8,128)S(1)} %bitcast.217, f32[12,9,128,128]{3,2,1,0:T(8,128)S(1)} %get-tuple-element.49, f32[12,128]{1,0:T(8,128)S(1)} %fusion.2, f32[12,128]{1,0:T(8,128)S(1)} %get-tuple-element.48, f32[9]{0:T(128)S(1)} %copy-done.31), kind=kOutput, calls=%fused_computation.30 | convolution fusion | flops 1366032384 | bytes 11022372 | tf_op jit(solution)/shard_map/bhqsk,bqhd->bskhd/dot_general | solution.py:107
  239.6 11.8 %bitcast_multiply_fusion = f32[12,128,9,128]{1,3,2,0:T(8,128)S(1)} fusion(f32[12,128]{1,0:T(8,128)S(1)} %bitcast.220, f32[128,12,64,1]{0,2,3,1:T(8,128)S(1)} %bitcast.218, f32[1,9,128,2,12,64]{2,5,1,4,3,0:T(8,128)S(1)} %bitcast.198, f32[12,128]{1,0:T(8,128)S(1)} %fusion.2, f32[12,128]{1,0:T(8,128)S(1)} %get-tuple-element.48, f32[9]{0:T(128)S(1)} %copy-done.31, ...), kind=kOutput, calls=%fused_computation.16 | convolution fusion | flops 1369571328 | bytes 18113024 | tf_op jit(solution)/shard_map/bqhd,bskhd->bhqsk/dot_general | solution.py:97
  251.5 8.5 %multiply_bitcast_fusion = f32[1,9,128,12,64]{2,4,1,3,0:T(8,128)S(1)} fusion(f32[12,128,9,128]{1,3,2,0:T(8,128)S(1)} %bitcast_multiply_fusion, f32[128,12,64,1]{0,2,3,1:T(8,128)S(1)} %bitcast.200), kind=kOutput, calls=%fused_computation.25 | convolution fusion | flops 1359839232 | bytes 11010048 | tf_op jit(solution)/shard_map/bhqsk,bqhd->bskhd/dot_general | solution.py:104
  283.7 9.5 %fusion.8 = f32[12,64,128]{2,1,0:T(8,128)} fusion(f32[12,128,9,128]{1,3,2,0:T(8,128)} %copy-done.1, f32[1,9,128,2,12,64]{2,5,1,4,3,0:T(8,128)} %constant_dynamic-update-slice_fusion.2), kind=kOutput, calls=%fused_computation.39 | convolution fusion | flops 1359052800 | bytes 11010048 | tf_op jit(solution)/shard_map/bhqsk,bskhd->bqhd/dot_general | solution.py:100
  295.1 6.6 %collective-permute-start.8 = (f32[128,1536]{1,0:T(8,128)}, f32[128,1536]{1,0:T(8,128)}, u32[]{:S(2)}, u32[]{:S(2)}) collective-permute-start(f32[128,1536]{1,0:T(8,128)} %get-tuple-element.25), channel_id=1, source_target_pairs={{0,1},{1,0},{2,3},{3,2},{4,5},{5,4},{6,7},{7,6},{8,9},{9,8},{10,11... | collective-permute-start | bytes 2359304 | tf_op jit(solution)/shard_map/ppermute | solution.py:17
  303.1 6.9 %collective-permute-done.11 = f32[128,1536]{1,0:T(8,128)} collective-permute-done((f32[128,1536]{1,0:T(8,128)}, f32[128,1536]{1,0:T(8,128)}, u32[]{:S(2)}, u32[]{:S(2)}) %collective-permute-start.11) | collective-permute-done | bytes 786464 | tf_op jit(solution)/shard_map/ppermute | solution.py:17
  311.9 27.4 %collective-permute-done.9 = f32[128,1536]{1,0:T(8,128)} collective-permute-done((f32[128,1536]{1,0:T(8,128)}, f32[128,1536]{1,0:T(8,128)}, u32[]{:S(2)}, u32[]{:S(2)}) %collective-permute-start.9) | collective-permute-done | bytes 786464 | tf_op jit(solution)/shard_map/ppermute | solution.py:17
  346.2 7.9 %collective-permute-start.10 = (f32[64,1536]{1,0:T(8,128)S(1)}, f32[64,1536]{1,0:T(8,128)S(1)}, u32[]{:S(2)}, u32[]{:S(2)}) collective-permute-start(f32[64,1536]{1,0:T(8,128)S(1)} %slice_select_fusion.6), channel_id=1, source_target_pairs={{0,1},{1,0},{2,3},{3,2},{4,5},{5,4},{6,7},{7,6},{8,9},{9,8},{10,11... | collective-permute-start | bytes 1179656 | tf_op jit(solution)/shard_map/ppermute | solution.py:17
  354.8 6.6 %collective-permute-done.18 = f32[128,1536]{1,0:T(8,128)S(1)} collective-permute-done((f32[128,1536]{1,0:T(8,128)}, f32[128,1536]{1,0:T(8,128)S(1)}, u32[]{:S(2)}, u32[]{:S(2)}) %collective-permute-start.18) | collective-permute-done | bytes 786464 | tf_op jit(solution)/shard_map/ppermute | solution.py:17
  363.4 14.3 %collective-permute-done.14 = f32[128,1536]{1,0:T(8,128)S(1)} collective-permute-done((f32[128,1536]{1,0:T(8,128)}, f32[128,1536]{1,0:T(8,128)S(1)}, u32[]{:S(2)}, u32[]{:S(2)}) %collective-permute-start.14) | collective-permute-done | bytes 786464 | tf_op jit(solution)/shard_map/ppermute | solution.py:17
  403.8 6.0 %collective-permute-done.15 = f32[64,1536]{1,0:T(8,128)S(1)} collective-permute-done((f32[64,1536]{1,0:T(8,128)}, f32[64,1536]{1,0:T(8,128)S(1)}, u32[]{:S(2)}, u32[]{:S(2)}) %collective-permute-start.15) | collective-permute-done | bytes 393248 | tf_op jit(solution)/shard_map/ppermute | solution.py:17
  414.4 5.3 %collective-permute-start.20 = (f32[32,1536]{1,0:T(8,128)}, f32[32,1536]{1,0:T(8,128)}, u32[]{:S(2)}, u32[]{:S(2)}) collective-permute-start(f32[32,1536]{1,0:T(8,128)} %slice_select_fusion.10), channel_id=1, source_target_pairs={{0,4},{1,5},{2,6},{3,7},{4,0},{5,1},{6,2},{7,3},{8,12},{9,13},{10,... | collective-permute-start | bytes 589832 | tf_op jit(solution)/shard_map/ppermute | solution.py:17
  444.9 5.9 %collective-permute-start.33 = (f32[8,1536]{1,0:T(8,128)S(1)}, f32[8,1536]{1,0:T(8,128)S(1)}, u32[]{:S(2)}, u32[]{:S(2)}) collective-permute-start(f32[8,1536]{1,0:T(8,128)S(1)} %slice_select_fusion.19), channel_id=1, source_target_pairs={{0,4},{1,5},{2,6},{3,7},{4,0},{5,1},{6,2},{7,3},{8,12},{9,13},{10,... | collective-permute-start | bytes 147464 | tf_op jit(solution)/shard_map/ppermute | solution.py:17
  458.5 5.5 %collective-permute-done.41 = f32[4,1536]{1,0:T(4,128)S(1)} collective-permute-done((f32[4,1536]{1,0:T(4,128)S(1)}, f32[4,1536]{1,0:T(4,128)S(1)}, u32[]{:S(2)}, u32[]{:S(2)}) %collective-permute-start.41) | collective-permute-done | bytes 24608 | tf_op jit(solution)/shard_map/ppermute | solution.py:17
  (266 shorter events, 173.6 us)
Async XLA Ops:
  2.7 19.5 %collective-permute-start = (f32[128,1536]{1,0:T(8,128)S(1)}, f32[128,1536]{1,0:T(8,128)S(1)}, u32[]{:S(2)}, u32[]{:S(2)}) collective-permute-start(f32[128,1536]{1,0:T(8,128)S(1)} %constant_dynamic-update-slice_fusion), channel_id=1, source_target_pairs={{0,1},{1,0},{2,3},{3,2},{4,5},{5,4},{6,7},{7,6},{8,9},{9,8},{10,11... | collective-permute-start | bytes 2359304 | tf_op jit(solution)/shard_map/ppermute | solution.py:17
  25.3 37.1 %collective-permute-start.1 = (f32[128,1536]{1,0:T(8,128)S(1)}, f32[128,1536]{1,0:T(8,128)S(1)}, u32[]{:S(2)}, u32[]{:S(2)}) collective-permute-start(f32[128,1536]{1,0:T(8,128)S(1)} %bitcast.215), channel_id=1, source_target_pairs={{0,2},{1,3},{2,0},{3,1},{4,6},{5,7},{6,4},{7,5},{8,10},{9,11},{10,... | collective-permute-start | bytes 2359304 | tf_op jit(solution)/shard_map/ppermute | solution.py:17
  65.3 40.7 %collective-permute-start.2 = (f32[128,1536]{1,0:T(8,128)S(1)}, f32[128,1536]{1,0:T(8,128)S(1)}, u32[]{:S(2)}, u32[]{:S(2)}) collective-permute-start(f32[128,1536]{1,0:T(8,128)S(1)} %bitcast.214), channel_id=1, source_target_pairs={{0,4},{1,5},{2,6},{3,7},{4,0},{5,1},{6,2},{7,3},{8,12},{9,13},{10,... | collective-permute-start | bytes 2359304 | tf_op jit(solution)/shard_map/ppermute | solution.py:17
  109.0 18.4 %collective-permute-start.3 = (f32[128,1536]{1,0:T(8,128)S(1)}, f32[128,1536]{1,0:T(8,128)S(1)}, u32[]{:S(2)}, u32[]{:S(2)}) collective-permute-start(f32[128,1536]{1,0:T(8,128)S(1)} %bitcast.211), channel_id=1, source_target_pairs={{0,8},{1,9},{2,10},{3,11},{4,12},{5,13},{6,14},{7,15},{8,0},{9,1},... | collective-permute-start | bytes 2359304 | tf_op jit(solution)/shard_map/ppermute | solution.py:17
  130.4 19.2 %collective-permute-start.4 = (f32[128,1536]{1,0:T(8,128)S(1)}, f32[128,1536]{1,0:T(8,128)S(1)}, u32[]{:S(2)}, u32[]{:S(2)}) collective-permute-start(f32[128,1536]{1,0:T(8,128)S(1)} %bitcast.212), channel_id=1, source_target_pairs={{0,16},{1,17},{2,18},{3,19},{4,20},{5,21},{6,22},{7,23},{8,24},{9,... | collective-permute-start | bytes 2359304 | tf_op jit(solution)/shard_map/ppermute | solution.py:17
  158.9 19.8 %collective-permute-start.6 = (f32[128,1536]{1,0:T(8,128)}, f32[128,1536]{1,0:T(8,128)S(1)}, u32[]{:S(2)}, u32[]{:S(2)}) collective-permute-start(f32[128,1536]{1,0:T(8,128)} %bitcast.189), channel_id=1, source_target_pairs={{0,64},{1,65},{2,66},{3,67},{4,68},{5,69},{6,70},{7,71},{8,72},{9,... | collective-permute-start | bytes 2359304 | tf_op jit(solution)/shard_map/ppermute | solution.py:17
  182.6 21.0 %collective-permute-start.7 = (f32[128,1536]{1,0:T(8,128)}, f32[128,1536]{1,0:T(8,128)}, u32[]{:S(2)}, u32[]{:S(2)}) collective-permute-start(f32[128,1536]{1,0:T(8,128)} %bitcast.188), channel_id=1, source_target_pairs={{0,128},{1,129},{2,130},{3,131},{4,132},{5,133},{6,134},{7,135},{8... | collective-permute-start | bytes 2359304 | tf_op jit(solution)/shard_map/ppermute | solution.py:17
  279.6 30.4 %collective-permute-start.11 = (f32[128,1536]{1,0:T(8,128)}, f32[128,1536]{1,0:T(8,128)}, u32[]{:S(2)}, u32[]{:S(2)}) collective-permute-start(f32[128,1536]{1,0:T(8,128)} %get-tuple-element.27), channel_id=1, source_target_pairs={{0,4},{1,5},{2,6},{3,7},{4,0},{5,1},{6,2},{7,3},{8,12},{9,13},{10,... | collective-permute-start | bytes 2359304 | tf_op jit(solution)/shard_map/ppermute | solution.py:17
  283.7 55.7 %collective-permute-start.9 = (f32[128,1536]{1,0:T(8,128)}, f32[128,1536]{1,0:T(8,128)}, u32[]{:S(2)}, u32[]{:S(2)}) collective-permute-start(f32[128,1536]{1,0:T(8,128)} %get-tuple-element.26), channel_id=1, source_target_pairs={{0,2},{1,3},{2,0},{3,1},{4,6},{5,7},{6,4},{7,5},{8,10},{9,11},{10,... | collective-permute-start | bytes 2359304 | tf_op jit(solution)/shard_map/ppermute | solution.py:17
  295.1 177.4 %collective-permute-start.8 = (f32[128,1536]{1,0:T(8,128)}, f32[128,1536]{1,0:T(8,128)}, u32[]{:S(2)}, u32[]{:S(2)}) collective-permute-start(f32[128,1536]{1,0:T(8,128)} %get-tuple-element.25), channel_id=1, source_target_pairs={{0,1},{1,0},{2,3},{3,2},{4,5},{5,4},{6,7},{7,6},{8,9},{9,8},{10,11... | collective-permute-start | bytes 2359304 | tf_op jit(solution)/shard_map/ppermute | solution.py:17
  301.7 42.0 %collective-permute-start.36 = (f32[128,1536]{1,0:T(8,128)}, f32[128,1536]{1,0:T(8,128)S(1)}, u32[]{:S(2)}, u32[]{:S(2)}) collective-permute-start(f32[128,1536]{1,0:T(8,128)} %get-tuple-element.30), channel_id=1, source_target_pairs={{0,128},{1,129},{2,130},{3,131},{4,132},{5,133},{6,134},{7,135},{8... | collective-permute-start | bytes 2359304 | tf_op jit(solution)/shard_map/ppermute | solution.py:17
  303.1 42.2 %collective-permute-start.29 = (f32[128,1536]{1,0:T(8,128)}, f32[128,1536]{1,0:T(8,128)S(1)}, u32[]{:S(2)}, u32[]{:S(2)}) collective-permute-start(f32[128,1536]{1,0:T(8,128)} %get-tuple-element.31), channel_id=1, source_target_pairs={{0,64},{1,65},{2,66},{3,67},{4,68},{5,69},{6,70},{7,71},{8,72},{9,... | collective-permute-start | bytes 2359304 | tf_op jit(solution)/shard_map/ppermute | solution.py:17
  310.0 36.1 %collective-permute-start.23 = (f32[128,1536]{1,0:T(8,128)}, f32[128,1536]{1,0:T(8,128)S(1)}, u32[]{:S(2)}, u32[]{:S(2)}) collective-permute-start(f32[128,1536]{1,0:T(8,128)} %get-tuple-element.29), channel_id=1, source_target_pairs={{0,32},{1,33},{2,34},{3,35},{4,36},{5,37},{6,38},{7,39},{8,40},{9,... | collective-permute-start | bytes 2359304 | tf_op jit(solution)/shard_map/ppermute | solution.py:17
  339.4 22.1 %collective-permute-start.18 = (f32[128,1536]{1,0:T(8,128)}, f32[128,1536]{1,0:T(8,128)S(1)}, u32[]{:S(2)}, u32[]{:S(2)}) collective-permute-start(f32[128,1536]{1,0:T(8,128)} %get-tuple-element.28), channel_id=1, source_target_pairs={{0,16},{1,17},{2,18},{3,19},{4,20},{5,21},{6,22},{7,23},{8,24},{9,... | collective-permute-start | bytes 2359304 | tf_op jit(solution)/shard_map/ppermute | solution.py:17
  343.7 34.0 %collective-permute-start.14 = (f32[128,1536]{1,0:T(8,128)}, f32[128,1536]{1,0:T(8,128)S(1)}, u32[]{:S(2)}, u32[]{:S(2)}) collective-permute-start(f32[128,1536]{1,0:T(8,128)} %get-tuple-element.24), channel_id=1, source_target_pairs={{0,8},{1,9},{2,10},{3,11},{4,12},{5,13},{6,14},{7,15},{8,0},{9,1},... | collective-permute-start | bytes 2359304 | tf_op jit(solution)/shard_map/ppermute | solution.py:17
  345.3 41.1 %collective-permute-start.12 = (f32[64,1536]{1,0:T(8,128)}, f32[64,1536]{1,0:T(8,128)}, u32[]{:S(2)}, u32[]{:S(2)}) collective-permute-start(f32[64,1536]{1,0:T(8,128)} %slice_select_fusion.5), channel_id=1, source_target_pairs={{0,2},{1,3},{2,0},{3,1},{4,6},{5,7},{6,4},{7,5},{8,10},{9,11},{10,... | collective-permute-start | bytes 1179656 | tf_op jit(solution)/shard_map/ppermute | solution.py:17
  346.2 33.3 %collective-permute-start.10 = (f32[64,1536]{1,0:T(8,128)S(1)}, f32[64,1536]{1,0:T(8,128)S(1)}, u32[]{:S(2)}, u32[]{:S(2)}) collective-permute-start(f32[64,1536]{1,0:T(8,128)S(1)} %slice_select_fusion.6), channel_id=1, source_target_pairs={{0,1},{1,0},{2,3},{3,2},{4,5},{5,4},{6,7},{7,6},{8,9},{9,8},{10,11... | collective-permute-start | bytes 1179656 | tf_op jit(solution)/shard_map/ppermute | solution.py:17
  361.5 26.4 %collective-permute-start.37 = (f32[64,1536]{1,0:T(8,128)}, f32[64,1536]{1,0:T(8,128)}, u32[]{:S(2)}, u32[]{:S(2)}) collective-permute-start(f32[64,1536]{1,0:T(8,128)} %slice_select_fusion), channel_id=1, source_target_pairs={{0,64},{1,65},{2,66},{3,67},{4,68},{5,69},{6,70},{7,71},{8,72},{9,... | collective-permute-start | bytes 1179656 | tf_op jit(solution)/shard_map/ppermute | solution.py:17
  387.9 21.9 %collective-permute-start.15 = (f32[64,1536]{1,0:T(8,128)}, f32[64,1536]{1,0:T(8,128)S(1)}, u32[]{:S(2)}, u32[]{:S(2)}) collective-permute-start(f32[64,1536]{1,0:T(8,128)} %slice_select_fusion.4), channel_id=1, source_target_pairs={{0,4},{1,5},{2,6},{3,7},{4,0},{5,1},{6,2},{7,3},{8,12},{9,13},{10,... | collective-permute-start | bytes 1179656 | tf_op jit(solution)/shard_map/ppermute | solution.py:17
  391.5 22.8 %collective-permute-start.13 = (f32[32,1536]{1,0:T(8,128)S(1)}, f32[32,1536]{1,0:T(8,128)S(1)}, u32[]{:S(2)}, u32[]{:S(2)}) collective-permute-start(f32[32,1536]{1,0:T(8,128)S(1)} %slice_select_fusion.12), channel_id=1, source_target_pairs={{0,1},{1,0},{2,3},{3,2},{4,5},{5,4},{6,7},{7,6},{8,9},{9,8},{10,11... | collective-permute-start | bytes 589832 | tf_op jit(solution)/shard_map/ppermute | solution.py:17
  395.9 23.7 %collective-permute-start.38 = (f32[32,1536]{1,0:T(8,128)S(1)}, f32[32,1536]{1,0:T(8,128)S(1)}, u32[]{:S(2)}, u32[]{:S(2)}) collective-permute-start(f32[32,1536]{1,0:T(8,128)S(1)} %slice_select_fusion.7), channel_id=1, source_target_pairs={{0,32},{1,33},{2,34},{3,35},{4,36},{5,37},{6,38},{7,39},{8,40},{9,... | collective-permute-start | bytes 589832 | tf_op jit(solution)/shard_map/ppermute | solution.py:17
  398.8 22.4 %collective-permute-start.31 = (f32[32,1536]{1,0:T(8,128)S(1)}, f32[32,1536]{1,0:T(8,128)S(1)}, u32[]{:S(2)}, u32[]{:S(2)}) collective-permute-start(f32[32,1536]{1,0:T(8,128)S(1)} %slice_select_fusion.8), channel_id=1, source_target_pairs={{0,16},{1,17},{2,18},{3,19},{4,20},{5,21},{6,22},{7,23},{8,24},{9,... | collective-permute-start | bytes 589832 | tf_op jit(solution)/shard_map/ppermute | solution.py:17
  409.8 19.4 %collective-permute-start.25 = (f32[32,1536]{1,0:T(8,128)}, f32[32,1536]{1,0:T(8,128)}, u32[]{:S(2)}, u32[]{:S(2)}) collective-permute-start(f32[32,1536]{1,0:T(8,128)} %slice_select_fusion.9), channel_id=1, source_target_pairs={{0,8},{1,9},{2,10},{3,11},{4,12},{5,13},{6,14},{7,15},{8,0},{9,1},... | collective-permute-start | bytes 589832 | tf_op jit(solution)/shard_map/ppermute | solution.py:17
  419.7 18.4 %collective-permute-start.16 = (f32[32,1536]{1,0:T(8,128)}, f32[32,1536]{1,0:T(8,128)}, u32[]{:S(2)}, u32[]{:S(2)}) collective-permute-start(f32[32,1536]{1,0:T(8,128)} %slice_select_fusion.11), channel_id=1, source_target_pairs={{0,2},{1,3},{2,0},{3,1},{4,6},{5,7},{6,4},{7,5},{8,10},{9,11},{10,... | collective-permute-start | bytes 589832 | tf_op jit(solution)/shard_map/ppermute | solution.py:17
  (54 other events, 657.6 us)
where the time goes:
time: 485 us; the launch traced here: 475 us
  waiting for transfers between devices  219 us (45%)
  starting transfers between devices  87 us (18%)
  local copies, waits for them, and re-layouts  66.5 us (14%)
  matrix products  62 us (13%)
  other arithmetic  39 us (8%)
    ppermute x44, waiting for transfers between devices, from_partner(): lax.ppermute(value, axis, [(i, i ^ 1 << distance) for i in range(lax.axis...  219 us
    ppermute x44, starting transfers between devices, from_partner(): lax.ppermute(value, axis, [(i, i ^ 1 << distance) for i in range(lax.axis...  87 us
    unnamed x88, local copies, waits for them, and re-layouts  27.1 us
    dot_general x1, matrix products, on_device(): jnp.einsum('bqhd,bskhd->bhqsk', query_heads, key_part, precision=HIGHEST_...  13.8 us
    dot_general x1, matrix products, on_device(): jnp.einsum('bqhd,bskhd->bhqsk', grad_heads, value_part, precision=HIGHEST...  11.8 us
    dot_general x1, matrix products, on_device(): jnp.einsum('bhqsk,bqhd->bskhd', weights, grad_heads, precision=HIGHEST_PR...  11.6 us
    add x21, other arithmetic, level_sweep(): moved = kept_half + from_partner(sent_half, ('seqhi', 'seqlo'), bit_number)  10.9 us
    select_n x28, other arithmetic, split_half(): sent_half = jnp.where(upper_half, matrix[:middle], matrix[middle:])  10.8 us
  transfers between devices with their start and end apart: 44, of which 18 were waited for; matrix products, arithmetic and copies ran while one was open for 13% of the time, Pallas kernels for 0%

commit v1 on v0

v1 whole, which is shorter than its diff:
```python
import functools
import math

import jax
import jax.numpy as jnp
from jax import lax
from jax.experimental import pallas as pl
from jax.experimental.pallas import tpu as pltpu
from jax.sharding import PartitionSpec as P

MESH = pl.DeviceIdType.MESH
F32 = jnp.float32
BF16 = jnp.bfloat16
HEADS = 12
HD = 64
B = 128
LOG_TWO = math.log(2.0)
NT = (((1,), (1,)), ((), ()))

OWN_A, OWN_B, C1_A, C1_B, C2_A, SIB_A, C2_O, SIB_B, SETS = 0, 8, 12, 16, 18, 20, 25, 26, 31


def dot(a, b, dims=(((1,), (0,)), ((), ()))):
    return lax.dot_general(a, b, dims, preferred_element_type=F32)


def split(v):
    hi = v.astype(BF16)
    return hi, (v - hi.astype(F32)).astype(BF16)


def rows(start, count):
    return pl.ds(pl.multiple_of(start, 8), count)


def kernel(
    q_ref, k_ref, v_ref, g_ref,
    oa_ref, oq_ref, ok_ref, ov_ref,
    kvs, qgs, kvr, qgr, c2o, cs3, cs4, cs5, cs6, cs7, sib,
    hl, hlt, xs, xt, sd, pdh, pdl, ga, xr, gs, gr, u3, u4, u5, u6, u7, rqa, fqa, fkv,
    kv_s, kv_r, qg_s, qg_r, cx_s, cx_r, sb_s, sb_r, gx_s, gx_r, gs_s, gs_r, rq_s, rq_r, rk_s, rk_r,
):
    hi_id, lo_id = lax.axis_index("seqhi"), lax.axis_index("seqlo")
    x, k = lax.div(hi_id, 2), lax.rem(hi_id, 2)
    y, z = lax.div(lo_id, 8), lax.rem(lo_id, 8)
    cw = lax.rem(z, 2)
    t = lax.div(z, 2)
    quad = lax.div(z, 4)
    p = x * 8 + cw * 4 + y
    other = (x * 2 + 1 - k, lo_id)
    here = cw == k

    def subtree_device(pp):
        xx, rest = lax.div(pp, 8), lax.rem(pp, 8)
        return (xx * 2 + k, lax.rem(rest, 4) * 8 + 2 * t + lax.div(rest, 4))

    barrier = pltpu.get_barrier_semaphore()

    def greet(dev):
        pl.semaphore_signal(barrier, inc=1, device_id=dev, device_id_type=MESH)

    def greet_ring(i, _):
        @pl.when(jnp.logical_not(here & (i == z)))
        def _():
            greet((x * 2 + cw, y * 8 + i))
        wk, wz = lax.rem(i, 2), 2 * lax.div(i, 2) + k

        @pl.when(jnp.logical_not((wk == k) & (wz == z)))
        def _():
            greet((x * 2 + wk, y * 8 + wz))
        return 0

    lax.fori_loop(0, 8, greet_ring, 0)
    greet(other)

    def greet_sub(i, _):
        greet(subtree_device(lax.rem(p + i, 32)))
        return 0

    lax.fori_loop(1, 32, greet_sub, 0)

    low = lax.broadcasted_iota(jnp.int32, (B, B), 1) < HD

    def pack(a_ref, b_ref, dst, scale):
        for pair in range(HEADS // 2):
            cols = slice(pair * B, (pair + 1) * B)
            a, b = a_ref[:, cols], b_ref[:, cols]
            if scale != 1.0:
                a = a * scale
            dst[2 * pair] = jnp.where(low, a, pltpu.roll(b, HD, 1))
            dst[2 * pair + 1] = jnp.where(low, pltpu.roll(a, HD, 1), b)

    pack(k_ref, v_ref, kvs, 1.0)
    pl.semaphore_wait(barrier, 48 - 2 * (1 - lax.rem(cw + k, 2)))

    def send_out(src, dst, ssem, rsem):
        def step(i, _):
            u = lax.rem(i + t, 4)
            wz = 2 * u + k
            for j in range(3):
                h = 3 * u + j
                wk = (0, quad, 1)[j]
                slot = z if j != 1 else 8 + lax.rem(z, 4)
                me = (wz == z) & (wk == k)

                @pl.when(me)
                def _():
                    pltpu.make_async_copy(src.at[h], dst.at[rows(slot * B, B)], rsem.at[slot]).start()

                @pl.when(jnp.logical_not(me))
                def _():
                    pltpu.make_async_remote_copy(
                        src.at[h], dst.at[rows(slot * B, B)], ssem.at[h], rsem.at[slot],
                        device_id=(x * 2 + wk, y * 8 + wz), device_id_type=MESH,
                    ).start()
            return 0

        lax.fori_loop(0, 4, step, 0)

    def sent_out(src, ssem):
        def step(u, _):
            wz = 2 * u + k
            for j in range(3):
                h = 3 * u + j
                wk = (0, quad, 1)[j]

                @pl.when(jnp.logical_not((wz == z) & (wk == k)))
                def _():
                    pltpu.make_async_copy(src.at[h], src.at[h], ssem.at[h]).wait()
            return 0

        lax.fori_loop(0, 4, step, 0)

    def landed(dst, rsem, slot):
        part = dst.at[rows(slot * B, B)]
        pltpu.make_async_copy(part, part, rsem.at[slot]).wait()

    def send_back(src, dst, ssem, rsem, slot, job):
        if job == 0:
            oz, h = slot, 3 * t + 2 * k
        else:
            oz, h = 4 * k + slot - OWN_B, 3 * t + 1
        me = here & (oz == z)
        part = src.at[rows(slot * B, B)]

        @pl.when(me)
        def _():
            pltpu.make_async_copy(part, dst.at[h], rsem.at[h]).start()

        @pl.when(jnp.logical_not(me))
        def _():
            pltpu.make_async_remote_copy(
                part, dst.at[h], ssem.at[slot], rsem.at[h],
                device_id=(x * 2 + cw, y * 8 + oz), device_id_type=MESH,
            ).start()

    def sent_back(src, ssem, slot, job):
        oz = slot if job == 0 else 4 * k + slot - OWN_B

        @pl.when(jnp.logical_not(here & (oz == z)))
        def _():
            part = src.at[rows(slot * B, B)]
            pltpu.make_async_copy(part, part, ssem.at[slot]).wait()

    def send_subtrees(m, src_part, dst, ssem, rsem):
        size = 2**m
        n = B // size
        group = lax.div(p, size)
        base = (group + 1 - 2 * lax.rem(group, 2)) * size
        mine = lax.rem(p, size) * n

        def step(i, _):
            j = lax.rem(i + p, size)
            pltpu.make_async_remote_copy(
                src_part(j, n), dst.at[m, :, rows(mine, n), :], ssem.at[m], rsem.at[m],
                device_id=subtree_device(base + j), device_id_type=MESH,
            ).start()
            return 0

        lax.fori_loop(0, size, step, 0)

    def wait_all(ref, sem):
        pltpu.make_async_copy(ref, ref, sem).wait()

    send_out(kvs, kvr, kv_s, kv_r)
    pack(q_ref, g_ref, qgs, 0.125)
    ga[...] = jnp.zeros_like(ga)
    sent_out(kvs, kv_s)
    send_out(qgs, qgr, qg_s, qg_r)

    def put(index, v):
        h, l = split(v)
        hl[index, :, 0:B] = h
        hl[index, :, B : 2 * B] = l
        th, tl = split(v.T)
        hlt[index, 0:B, :] = th
        hlt[index, B : 2 * B, :] = tl

    def halve(ref, start, n):
        return 0.5 * (ref[pl.ds(start, n, stride=2), :] + ref[pl.ds(start + 1, n, stride=2), :])

    for s in range(OWN_B, 12):
        landed(kvr, kv_r, s)
    for i in range(2):
        kvr[(C1_B + i) * B : (C1_B + i + 1) * B] = halve(kvr, (OWN_B + 2 * i) * B, B)
    kvr[30 * B : 31 * B] = halve(kvr, C1_B * B, B)
    c2_mine = kvr.at[pl.ds(30 * B, B)]
    cx = pltpu.make_async_remote_copy(c2_mine, c2o, cx_s, cx_r, device_id=other, device_id_type=MESH)
    cx.start()
    for s in range(8):
        landed(kvr, kv_r, s)
    for i in range(4):
        kvr[(C1_A + i) * B : (C1_A + i + 1) * B] = halve(kvr, (OWN_A + 2 * i) * B, B)
    for i in range(2):
        kvr[(C2_A + i) * B : (C2_A + i + 1) * B] = halve(kvr, (C1_A + 2 * i) * B, B)
    cs3[0] = halve(kvr, C2_A * B, B)
    cs3[1, rows(64 * k, 64), :] = halve(kvr, 30 * B, 64)
    cx.wait_recv()
    cs3[1, rows(64 * (1 - k), 64), :] = halve(c2o, 0, 64)
    levels = (cs3, cs4, cs5, cs6, cs7)
    for m in range(5):
        if m:
            for job in range(2):
                levels[m][job] = halve(levels[m - 1].at[job], 0, B >> m)
        send_subtrees(m, lambda j, n: levels[m], sib, sb_s, sb_r)

    def put_step(i, _):
        put(i, kvr[rows(i * B, B), :])
        return 0

    lax.fori_loop(0, 20, put_step, 0)
    put(C2_O, c2o[...])
    for m in range(5):
        wait_all(sib.at[m], sb_r.at[m])

    def put_sib(m, _):
        put(SIB_A + m, sib[m, 0])
        put(SIB_B + m, sib[m, 1])
        return 0

    lax.fori_loop(0, 5, put_sib, 0)

    def load_set(position, index):
        part = slice(position * B, (position + 1) * B)
        h = hl[index, :, 0:B]
        xs[part, 0:B] = h
        xs[part, B : 2 * B] = hl[index, :, B : 2 * B]
        xs[part, 2 * B : 3 * B] = h
        xt[:, part] = hlt[index]

    def flip(i):
        return i + 1 - 2 * lax.rem(i, 2)

    def run_task(b, job):
        own, c1, sibs = ((OWN_A, C1_A, SIB_A), (OWN_B, C1_B, SIB_B))[job]
        slot = own + b
        indices = [slot, own + flip(b), c1 + flip(lax.div(b, 2))]
        indices.append(C2_A + flip(lax.div(b, 4)) if job == 0 else C2_O)
        indices += [sibs + m for m in range(5)]
        for position in range(4):
            load_set(position, indices[position])
        landed(qgr, qg_r, slot)
        qh, ql = split(qgr[rows(slot * B, B), :])
        zero = jnp.zeros_like(qh)
        wide = jnp.concatenate(
            [
                jnp.concatenate([jnp.where(low, qh, zero), jnp.where(low, ql, zero)], axis=1),
                jnp.concatenate([jnp.where(low, zero, qh), jnp.where(low, zero, ql)], axis=1),
            ],
            axis=0,
        )
        w = jnp.concatenate([wide[:, 0:B], wide], axis=1)
        sd[...] = dot(xs[...], w, NT)
        top = jnp.full((8, B), -jnp.inf, F32)
        offsets = [max(i - 1, 0) * LOG_TWO for i in range(9)]
        for i in range(9):
            s = sd[i * B : (i + 1) * B, 0:B]
            top = jnp.maximum(top, jnp.max(s.reshape(16, 8, B), axis=0) + offsets[i])
        top = jnp.max(top, axis=0, keepdims=True)
        total = jnp.zeros((8, B), F32)
        along = jnp.zeros((8, B), F32)
        for i in range(9):
            part = slice(i * B, (i + 1) * B)
            e = jnp.exp(sd[part, 0:B] - (top - offsets[i]))
            sd[part, 0:B] = e
            total = total + jnp.sum(e.reshape(16, 8, B), axis=0)
            along = along + jnp.sum((e * sd[part, B : 2 * B]).reshape(16, 8, B), axis=0)
        norm = 1.0 / jnp.sum(total, axis=0, keepdims=True)
        row_dot = jnp.sum(along, axis=0, keepdims=True) * norm
        for i in range(9):
            part = slice(i * B, (i + 1) * B)
            prob = sd[part, 0:B] * norm
            ds = prob * (sd[part, B : 2 * B] - row_dot)
            pdh[part, 0:B], pdl[part, 0:B] = split(ds)
            pdh[part, B : 2 * B], pdl[part, B : 2 * B] = split(prob)
        high = pdh[...]
        out = dot(xt[...], high)
        out = out[0:B] + out[B : 2 * B] + dot(xt[0:B], pdl[...])
        both = jnp.concatenate([out[0:HD, 0:B] * 0.125, out[HD : 2 * HD, B : 2 * B]], axis=0)
        rqa[rows(slot * B, B), :] = both.T
        send_back(rqa, fqa, rq_s, rq_r, slot, job)
        sd[...] = dot(high, wide)
        grads = dot(pdl[...], wide[:, 0:B])
        for i in range(9):
            part = slice(i * B, (i + 1) * B)
            dst = rows(indices[i] * B, B)
            ga[dst, :] = ga[dst, :] + (sd[part, 0:B] + sd[part, B : 2 * B] + grads[part])

    def run_job(job, count):
        for m in range(5):
            load_set(4 + m, (SIB_A, SIB_B)[job] + m)

        def step(b, _):
            run_task(b, job)
            return 0

        lax.fori_loop(0, count, step, 0)

    run_job(1, 4)
    gx_src = ga.at[pl.ds(C2_O * B, 6 * B)]
    gx = pltpu.make_async_remote_copy(gx_src, xr, gx_s, gx_r, device_id=other, device_id_type=MESH)
    gx.start()
    run_job(0, 8)
    gx.wait()
    for m in range(5):
        gs[m, 0] = ga[(SIB_A + m) * B : (SIB_A + m + 1) * B]
        gs[m, 1] = ga[(SIB_B + m) * B : (SIB_B + m + 1) * B] + xr[(1 + m) * B : (2 + m) * B]
        send_subtrees(m, lambda j, n: gs.at[m, :, rows(j * n, n), :], gr, gs_s, gs_r)

    ups = (u3, u4, u5, u6, u7)
    for m in (4, 3, 2, 1, 0):
        wait_all(gr.at[m], gs_r.at[m])
        n = B >> m
        for job in range(2):
            acc = gr[m, job, 0:n]
            for j in range(1, 2**m):
                acc = acc + gr[m, job, j * n : (j + 1) * n]
            ups[m][job] = acc

    def spread(src, dst, start, n):
        half = 0.5 * src
        for odd in range(2):
            at = pl.ds(start + odd, n, stride=2)
            dst[at, :] = dst[at, :] + half

    for m in (4, 3, 2, 1):
        for job in range(2):
            spread(ups[m][job], ups[m - 1].at[job], 0, B >> m)
    spread(u3[0], ga, C2_A * B, B)
    for i in range(2):
        spread(ga[(C2_A + i) * B : (C2_A + i + 1) * B], ga, (C1_A + 2 * i) * B, B)
    for i in range(4):
        spread(ga[(C1_A + i) * B : (C1_A + i + 1) * B], ga, (OWN_A + 2 * i) * B, B)
    spread(u3[1, rows(64 * k, 64), :], xr, 0, 64)
    spread(xr[0:B], ga, C1_B * B, B)
    for i in range(2):
        spread(ga[(C1_B + i) * B : (C1_B + i + 1) * B], ga, (OWN_B + 2 * i) * B, B)

    def back_a(i, _):
        send_back(ga, fkv, rk_s, rk_r, i, 0)
        return 0

    def back_b(i, _):
        send_back(ga, fkv, rk_s, rk_r, i, 1)
        return 0

    lax.fori_loop(0, 8, back_a, 0)
    lax.fori_loop(8, 12, back_b, 0)

    def unpack(src, rsem, first_ref, last_ref):
        for pair in range(HEADS // 2):
            for h in (2 * pair, 2 * pair + 1):
                pltpu.make_async_copy(src.at[h], src.at[h], rsem.at[h]).wait()
            even, odd = src[2 * pair], src[2 * pair + 1]
            cols = slice(pair * B, (pair + 1) * B)
            first_ref[:, cols] = jnp.where(low, even, pltpu.roll(odd, HD, 1))
            last_ref[:, cols] = jnp.where(low, pltpu.roll(even, HD, 1), odd)

    unpack(fqa, rq_r, oq_ref, oa_ref)
    unpack(fkv, rk_r, ok_ref, ov_ref)

    sent_out(qgs, qg_s)
    cx.wait_send()
    for m in range(5):
        wait_all(sib.at[m], sb_s.at[m])
        wait_all(gr.at[m], gs_s.at[m])

    def done_a(i, _):
        sent_back(rqa, rq_s, i, 0)
        sent_back(ga, rk_s, i, 0)
        return 0

    def done_b(i, _):
        sent_back(rqa, rq_s, i, 1)
        sent_back(ga, rk_s, i, 1)
        return 0

    lax.fori_loop(0, 8, done_a, 0)
    lax.fori_loop(8, 12, done_b, 0)


def on_device(queries, keys, values, cotangent):
    shape = jax.ShapeDtypeStruct(queries.shape, F32)
    vm = pl.BlockSpec(memory_space=pltpu.VMEM)
    dma = pltpu.SemaphoreType.DMA
    scratch = [
        pltpu.VMEM((12, B, B), F32),
        pltpu.VMEM((12, B, B), F32),
        pltpu.VMEM((SETS * B, B), F32),
        pltpu.VMEM((12 * B, B), F32),
        pltpu.VMEM((B, B), F32),
    ]
    scratch += [pltpu.VMEM((2, B >> m, B), F32) for m in range(5)]
    scratch += [
        pltpu.VMEM((5, 2, B, B), F32),
        pltpu.VMEM((SETS, B, 2 * B), BF16),
        pltpu.VMEM((SETS, 2 * B, B), BF16),
        pltpu.VMEM((9 * B, 3 * B), BF16),
        pltpu.VMEM((2 * B, 9 * B), BF16),
        pltpu.VMEM((9 * B, 2 * B), F32),
        pltpu.VMEM((9 * B, 2 * B), BF16),
        pltpu.VMEM((9 * B, 2 * B), BF16),
        pltpu.VMEM((SETS * B, B), F32),
        pltpu.VMEM((6 * B, B), F32),
        pltpu.VMEM((5, 2, B, B), F32),
        pltpu.VMEM((5, 2, B, B), F32),
    ]
    scratch += [pltpu.VMEM((2, B >> m, B), F32) for m in range(5)]
    scratch += [
        pltpu.VMEM((12 * B, B), F32),
        pltpu.VMEM((12, B, B), F32),
        pltpu.VMEM((12, B, B), F32),
    ]
    scratch += [dma((12,))] * 4 + [dma] * 2 + [dma((5,))] * 2 + [dma] * 2 + [dma((5,))] * 2 + [dma((12,))] * 4
    return pl.pallas_call(
        kernel,
        out_shape=[shape] * 4,
        in_specs=[vm] * 4,
        out_specs=[vm] * 4,
        scratch_shapes=scratch,
        compiler_params=pltpu.CompilerParams(
            collective_id=0, has_side_effects=True, vmem_limit_bytes=56 * 2**20
        ),
    )(queries, keys, values, cotangent)


def solution(mesh):
    spec = P(("seqhi", "seqlo"), None)
    return jax.shard_map(
        on_device, mesh=mesh, in_specs=(spec,) * 4, out_specs=(spec,) * 4, check_vma=False
    )
```

time: 485 us -> 125 us (0.26)
  the two profiles are of different devices: /device:TPU:6 before, /device:TPU:9 now
where the time goes in v1:
time: 125 us
  Pallas kernels  119 us (95%)
  local copies, waits for them, and re-layouts  4.84 us (4%)
    pallas_call x1, Pallas kernels, on_device(): pl.pallas_call(kernel, out_shape=[shape] * 4, in_specs=[vm] * 4, out_spec...  119 us
    unnamed x10, local copies, waits for them, and re-layouts  4.84 us

profile of v1, /device:TPU:9, one launch (start us, length us, event | category | flops | bytes accessed | tf_op | source)
XLA Modules:
  0.0 124.8 jit_solution(14258979734691584045)
XLA Ops:
  0.6 119.3 %shard_map.75 = (f32[128,768]{1,0:T(8,128)}, f32[128,768]{1,0:T(8,128)}, f32[128,768]{1,0:T(8,128)}, f32[128,768]{1,0:T(8,128)}) custom-call(f32[128,768]{1,0:T(8,128)} %q_ref.1, f32[128,768]{1,0:T(8,128)} %k_ref.1, f32[128,768]{1,0:T(8,128)} %v_ref.1, f32[128,768]{1,0:T(8,128)} %g_ref.1), custom_call_target="tpu_custom_call" | custom-call | tf_op jit(solution)/shard_map/pallas_call | solution.py:435
  120.0 0.0 copy-start.2
  120.0 1.8 %copy.12 = f32[128,768]{1,0:T(8,128)} copy(f32[128,768]{1,0:T(8,128)} %get-tuple-element.8) | data formatting | bytes 786432
  121.8 0.0 copy-done.2
  121.8 0.0 copy-start.1
  121.8 0.7 copy.13
  122.6 0.4 copy-done.1
  123.0 0.0 copy-start
  123.0 0.7 copy.14
  123.7 0.4 copy-done
  124.1 0.7 copy.15
Async XLA Ops:
  120.0 1.8 %copy-start.2 = (f32[128,768]{1,0:T(8,128)S(1)}, f32[128,768]{1,0:T(8,128)}, u32[]{:S(2)}) copy-start(f32[128,768]{1,0:T(8,128)} %get-tuple-element.9) | copy-start | bytes 1179652
  121.8 1.1 copy-start.1
  123.0 1.1 copy-start

commit v2 on v1

v2 whole, which is shorter than its diff:
```python
import functools
import math

import jax
import jax.numpy as jnp
from jax import lax
from jax.experimental import pallas as pl
from jax.experimental.pallas import tpu as pltpu
from jax.sharding import PartitionSpec as P

MESH = pl.DeviceIdType.MESH
F32 = jnp.float32
BF16 = jnp.bfloat16
HEADS = 12
HD = 64
B = 128
LOG_TWO = math.log(2.0)
NT = (((1,), (1,)), ((), ()))

OWN_A, OWN_B, C1_A, C1_B, C2_A, SIB_A, C2_O, SIB_B, SETS = 0, 8, 12, 16, 18, 20, 25, 26, 31


def dot(a, b, dims=(((1,), (0,)), ((), ()))):
    return lax.dot_general(a, b, dims, preferred_element_type=F32)


def split(v):
    hi = v.astype(BF16)
    return hi, (v - hi.astype(F32)).astype(BF16)


def rows(start, count):
    return pl.ds(pl.multiple_of(start, 8), count)


def kernel(
    q_hbm, k_hbm, v_hbm, g_hbm,
    fqa, fkv, fc3,
    q_ref, k_ref, v_ref, g_ref,
    kvs, qgs, kvr, qgr, c2o, cs3, cs4, cs5, cs6, cs7, sib,
    hl, hlt, xs, xt, sd, dp, ph, plo, dh, dl, ga, xr, gs, gr, u3, u4, u5, u6, u7, rqa,
    in_s, kv_s, kv_r, qg_s, qg_r, cx_s, cx_r, sb_s, sb_r, gx_s, gx_r, gs_s, gs_r,
    rq_s, rq_r, rk_s, rk_r, rc_s, rc_r,
):
    hi_id, lo_id = lax.axis_index("seqhi"), lax.axis_index("seqlo")
    x, k = lax.div(hi_id, 2), lax.rem(hi_id, 2)
    y, z = lax.div(lo_id, 8), lax.rem(lo_id, 8)
    cw = lax.rem(z, 2)
    t = lax.div(z, 2)
    quad = lax.div(z, 4)
    p = x * 8 + cw * 4 + y
    other = (x * 2 + 1 - k, lo_id)
    here = cw == k

    def subtree_device(pp):
        xx, rest = lax.div(pp, 8), lax.rem(pp, 8)
        return (xx * 2 + k, lax.rem(rest, 4) * 8 + 2 * t + lax.div(rest, 4))

    loads = [
        pltpu.make_async_copy(src, dst, in_s.at[i])
        for i, (src, dst) in enumerate(((k_hbm, k_ref), (v_hbm, v_ref), (q_hbm, q_ref), (g_hbm, g_ref)))
    ]
    for load in loads:
        load.start()

    barrier = pltpu.get_barrier_semaphore()

    def greet(dev):
        pl.semaphore_signal(barrier, inc=1, device_id=dev, device_id_type=MESH)

    def greet_ring(i, _):
        @pl.when(jnp.logical_not(here & (i == z)))
        def _():
            greet((x * 2 + cw, y * 8 + i))
        wk, wz = lax.rem(i, 2), 2 * lax.div(i, 2) + k

        @pl.when(jnp.logical_not((wk == k) & (wz == z)))
        def _():
            greet((x * 2 + wk, y * 8 + wz))
        return 0

    lax.fori_loop(0, 8, greet_ring, 0)
    greet(other)

    def greet_sub(i, _):
        greet(subtree_device(lax.rem(p + i, 32)))
        return 0

    lax.fori_loop(1, 32, greet_sub, 0)

    low = lax.broadcasted_iota(jnp.int32, (B, B), 1) < HD

    def pack(a_ref, b_ref, dst, scale):
        for pair in range(HEADS // 2):
            cols = slice(pair * B, (pair + 1) * B)
            a, b = a_ref[:, cols], b_ref[:, cols]
            if scale != 1.0:
                a = a * scale
            dst[2 * pair] = jnp.where(low, a, pltpu.roll(b, HD, 1))
            dst[2 * pair + 1] = jnp.where(low, pltpu.roll(a, HD, 1), b)

    loads[0].wait()
    loads[1].wait()
    pack(k_ref, v_ref, kvs, 1.0)
    pl.semaphore_wait(barrier, 48 - 2 * (1 - lax.rem(cw + k, 2)))

    def send_out(src, dst, ssem, rsem, heads):
        def step(i, _):
            u = lax.rem(i + t, 4)
            wz = 2 * u + k
            for j in heads:
                h = 3 * u + j
                wk = (0, quad, 1)[j]
                slot = z if j != 1 else 8 + lax.rem(z, 4)
                me = (wz == z) & (wk == k)

                @pl.when(me)
                def _():
                    pltpu.make_async_copy(src.at[h], dst.at[rows(slot * B, B)], rsem.at[slot]).start()

                @pl.when(jnp.logical_not(me))
                def _():
                    pltpu.make_async_remote_copy(
                        src.at[h], dst.at[rows(slot * B, B)], ssem.at[h], rsem.at[slot],
                        device_id=(x * 2 + wk, y * 8 + wz), device_id_type=MESH,
                    ).start()
            return 0

        lax.fori_loop(0, 4, step, 0)

    def sent_out(src, ssem):
        def step(u, _):
            wz = 2 * u + k
            for j in range(3):
                h = 3 * u + j
                wk = (0, quad, 1)[j]

                @pl.when(jnp.logical_not((wz == z) & (wk == k)))
                def _():
                    pltpu.make_async_copy(src.at[h], src.at[h], ssem.at[h]).wait()
            return 0

        lax.fori_loop(0, 4, step, 0)

    def landed(dst, rsem, slot):
        part = dst.at[rows(slot * B, B)]
        pltpu.make_async_copy(part, part, rsem.at[slot]).wait()

    def owner(slot, job):
        if job == 0:
            return slot, 3 * t + 2 * k
        return 4 * k + slot - OWN_B, 3 * t + 1

    def send_back(part, dst, ssem, rsem, slot, job):
        oz, h = owner(slot, job)
        me = here & (oz == z)

        @pl.when(me)
        def _():
            pltpu.make_async_copy(part, dst.at[h], rsem.at[h]).start()

        @pl.when(jnp.logical_not(me))
        def _():
            pltpu.make_async_remote_copy(
                part, dst.at[h], ssem.at[slot], rsem.at[h],
                device_id=(x * 2 + cw, y * 8 + oz), device_id_type=MESH,
            ).start()

    def sent_back(part, ssem, slot, job):
        oz, _ = owner(slot, job)

        @pl.when(jnp.logical_not(here & (oz == z)))
        def _():
            pltpu.make_async_copy(part, part, ssem.at[slot]).wait()

    def block(ref, slot):
        return ref.at[rows(slot * B, B)]

    def c3_part(slot, job):
        return u3.at[job, rows(16 * owner(slot, job)[0], 16), :]

    def both_jobs(what):
        for job, (first, last) in enumerate(((0, 8), (8, 12))):
            def step(i, _, job=job):
                what(i, job)
                return 0

            lax.fori_loop(first, last, step, 0)

    def send_subtrees(m, src_part, dst, ssem, rsem):
        size = 2**m
        n = B // size
        group = lax.div(p, size)
        base = (group + 1 - 2 * lax.rem(group, 2)) * size
        mine = lax.rem(p, size) * n

        def step(i, _):
            j = lax.rem(i + p, size)
            pltpu.make_async_remote_copy(
                src_part(j, n), dst.at[m, :, rows(mine, n), :], ssem.at[m], rsem.at[m],
                device_id=subtree_device(base + j), device_id_type=MESH,
            ).start()
            return 0

        lax.fori_loop(0, size, step, 0)

    def wait_all(ref, sem):
        pltpu.make_async_copy(ref, ref, sem).wait()

    send_out(kvs, kvr, kv_s, kv_r, (1, 0, 2))
    loads[2].wait()
    loads[3].wait()
    pack(q_ref, g_ref, qgs, 0.125)
    for start, count in ((C2_A, SETS - C2_A),):
        ga[start * B : (start + count) * B] = jnp.zeros((count * B, B), F32)
    sent_out(kvs, kv_s)
    send_out(qgs, qgr, qg_s, qg_r, (1,))

    def put(index, v):
        h = v.astype(BF16)
        hf = h.astype(F32)
        l = v - hf
        kk = jnp.where(low, hf, pltpu.roll(l, HD, 1))
        vv = jnp.where(low, pltpu.roll(hf, HD, 1), l)
        hl[index, :, 0:B] = kk.astype(BF16)
        hl[index, :, B : 2 * B] = h
        hl[index, :, 2 * B : 3 * B] = vv.astype(BF16)
        hlt[index, 0:B, :] = kk.T.astype(BF16)
        hlt[index, B : 2 * B, :] = vv.T.astype(BF16)

    def halve(ref, start, n):
        return 0.5 * (ref[pl.ds(start, n, stride=2), :] + ref[pl.ds(start + 1, n, stride=2), :])

    for s in range(OWN_B, 12):
        landed(kvr, kv_r, s)
    for i in range(2):
        kvr[(C1_B + i) * B : (C1_B + i + 1) * B] = halve(kvr, (OWN_B + 2 * i) * B, B)
    kvr[30 * B : 31 * B] = halve(kvr, C1_B * B, B)
    c2_mine = kvr.at[pl.ds(30 * B, B)]
    cx = pltpu.make_async_remote_copy(c2_mine, c2o, cx_s, cx_r, device_id=other, device_id_type=MESH)
    cx.start()
    for s in range(8):
        landed(kvr, kv_r, s)
    for i in range(4):
        kvr[(C1_A + i) * B : (C1_A + i + 1) * B] = halve(kvr, (OWN_A + 2 * i) * B, B)
    for i in range(2):
        kvr[(C2_A + i) * B : (C2_A + i + 1) * B] = halve(kvr, (C1_A + 2 * i) * B, B)
    cs3[0] = halve(kvr, C2_A * B, B)
    cs3[1, rows(64 * k, 64), :] = halve(kvr, 30 * B, 64)
    cx.wait_recv()
    cs3[1, rows(64 * (1 - k), 64), :] = halve(c2o, 0, 64)
    levels = (cs3, cs4, cs5, cs6, cs7)
    for m in range(5):
        if m:
            for job in range(2):
                levels[m][job] = halve(levels[m - 1].at[job], 0, B >> m)
        send_subtrees(m, lambda j, n: levels[m], sib, sb_s, sb_r)
    send_out(qgs, qgr, qg_s, qg_r, (0, 2))

    def put_step(i, _):
        put(i, kvr[rows(i * B, B), :])
        return 0

    lax.fori_loop(0, 20, put_step, 0)
    put(C2_O, c2o[...])
    for m in range(5):
        wait_all(sib.at[m], sb_r.at[m])

    def put_sib(m, _):
        put(SIB_A + m, sib[m, 0])
        put(SIB_B + m, sib[m, 1])
        return 0

    lax.fori_loop(0, 5, put_sib, 0)

    def load_set(position, index):
        part = slice(position * B, (position + 1) * B)
        xs[part, :] = hl[index]
        xt[:, part] = hlt[index]

    def flip(i):
        return i + 1 - 2 * lax.rem(i, 2)

    low2 = lax.broadcasted_iota(jnp.int32, (2 * B, B), 1) < HD

    def run_pair(b, job):
        own, c1 = ((OWN_A, C1_A), (OWN_B, C1_B))[job]
        first = own + 2 * b
        side = c1 + flip(b)
        far = C2_A + flip(lax.div(b, 2)) if job == 0 else C2_O
        load_set(0, first)
        load_set(1, first + 1)
        load_set(2, side)
        load_set(3, far)
        landed(qgr, qg_r, first)
        landed(qgr, qg_r, first + 1)
        qg = qgr[rows(first * B, 2 * B), :]
        zero = jnp.zeros_like(qg)

        def halves(v):
            h = v.astype(BF16).astype(F32)
            return h, v - h

        h, l = halves(jnp.where(low2, qg * math.log2(math.e), qg))
        turned = pltpu.roll(h, HD, 1)
        rq = jnp.concatenate([jnp.where(low2, h, turned), jnp.where(low2, l, zero)], axis=1).astype(BF16)
        rg = jnp.concatenate([jnp.where(low2, zero, l), jnp.where(low2, turned, h)], axis=1).astype(BF16)
        sd[...] = dot(xs[:, 0 : 2 * B], rq, NT)
        dp[...] = dot(xs[:, B : 3 * B], rg, NT)
        top = jnp.full((8, 2 * B), -jnp.inf, F32)
        offsets = [float(max(i - 1, 0)) for i in range(9)]
        for i in range(9):
            s = sd[i * B : (i + 1) * B]
            top = jnp.maximum(top, jnp.max(s.reshape(16, 8, 2 * B), axis=0) + offsets[i])
        top = jnp.max(top, axis=0, keepdims=True)
        total = jnp.zeros((8, 2 * B), F32)
        along = jnp.zeros((8, 2 * B), F32)
        for i in range(9):
            part = slice(i * B, (i + 1) * B)
            e = jnp.exp2(sd[part] - (top - offsets[i]))
            sd[part] = e
            total = total + jnp.sum(e.reshape(16, 8, 2 * B), axis=0)
            along = along + jnp.sum((e * dp[part]).reshape(16, 8, 2 * B), axis=0)
        norm = 1.0 / jnp.sum(total, axis=0, keepdims=True)
        row_dot = jnp.sum(along, axis=0, keepdims=True) * norm
        for i in range(9):
            part = slice(i * B, (i + 1) * B)
            prob = sd[part] * norm
            ph[part], plo[part] = split(prob)
            dh[part], dl[part] = split(prob * (dp[part] - row_dot))

        dq = dot(xt[0:B], dh[...])
        dq = dq[0:HD] + dq[HD:B] + dot(xt[0:HD], dl[...])
        at = dot(xt[B : 2 * B], ph[...])
        at = at[0:HD] + at[HD:B] + dot(xt[B : B + HD], plo[...])
        rqa[rows(first * B, 2 * B), :] = jnp.concatenate([dq * 0.125, at], axis=0).T
        for s in range(2):
            send_back(block(rqa, first + s), fqa, rq_s, rq_r, first + s, job)

        h, l = halves(qg)
        rk = jnp.concatenate([jnp.where(low2, h, zero), jnp.where(low2, l, zero)], axis=1).astype(BF16)
        rv = jnp.concatenate([jnp.where(low2, zero, h), jnp.where(low2, zero, l)], axis=1).astype(BF16)
        high = dot(dh[...], rk) + dot(ph[...], rv)
        grads = high[:, 0:B] + high[:, B : 2 * B] + (dot(dl[...], rk[:, 0:B]) + dot(plo[...], rv[:, 0:B]))
        ga[rows(first * B, 2 * B), :] = grads[0 : 2 * B]
        ga[rows(side * B, B), :] = grads[2 * B : 3 * B]
        ga[rows(far * B, B), :] = ga[rows(far * B, B), :] + grads[3 * B : 4 * B]
        top_sets = slice((SIB_A, SIB_B)[job] * B, ((SIB_A, SIB_B)[job] + 5) * B)
        ga[top_sets] = ga[top_sets] + grads[4 * B :]

    def run_job(job, count):
        for m in range(5):
            load_set(4 + m, (SIB_A, SIB_B)[job] + m)

        def step(i, _):
            run_pair(i if job else lax.rem(t + 4 - i, 4), job)
            return 0

        lax.fori_loop(0, count, step, 0)

    def spread(src, dst, start, n):
        half = 0.5 * src
        for odd in range(2):
            at = pl.ds(start + odd, n, stride=2)
            dst[at, :] = dst[at, :] + half

    run_job(1, 2)
    gx_src = ga.at[pl.ds(C2_O * B, 6 * B)]
    gx = pltpu.make_async_remote_copy(gx_src, xr, gx_s, gx_r, device_id=other, device_id_type=MESH)
    gx.start()
    run_job(0, 4)
    gx.wait()
    for m in range(5):
        gs[m, 0] = ga[(SIB_A + m) * B : (SIB_A + m + 1) * B]
        gs[m, 1] = ga[(SIB_B + m) * B : (SIB_B + m + 1) * B] + xr[(1 + m) * B : (2 + m) * B]
        send_subtrees(m, lambda j, n: gs.at[m, :, rows(j * n, n), :], gr, gs_s, gs_r)

    for i in range(2):
        spread(ga[(C2_A + i) * B : (C2_A + i + 1) * B], ga, (C1_A + 2 * i) * B, B)
    for i in range(4):
        spread(ga[(C1_A + i) * B : (C1_A + i + 1) * B], ga, (OWN_A + 2 * i) * B, B)
    spread(xr[0:B], ga, C1_B * B, B)
    for i in range(2):
        spread(ga[(C1_B + i) * B : (C1_B + i + 1) * B], ga, (OWN_B + 2 * i) * B, B)
    both_jobs(lambda i, job: send_back(block(ga, i), fkv, rk_s, rk_r, i, job))

    ups = (u3, u4, u5, u6, u7)
    for m in (4, 3, 2, 1, 0):
        wait_all(gr.at[m], gs_r.at[m])
        n = B >> m
        for job in range(2):
            acc = gr[m, job, 0:n]
            for j in range(1, 2**m):
                acc = acc + gr[m, job, j * n : (j + 1) * n]
            ups[m][job] = acc
    for m in (4, 3, 2, 1):
        for job in range(2):
            spread(ups[m][job], ups[m - 1].at[job], 0, B >> m)
    both_jobs(lambda i, job: send_back(c3_part(i, job), fc3, rc_s, rc_r, i, job))

    sent_out(qgs, qg_s)
    cx.wait_send()
    for m in range(5):
        wait_all(sib.at[m], sb_s.at[m])
        wait_all(gr.at[m], gs_s.at[m])

    def finish(i, job):
        sent_back(block(rqa, i), rq_s, i, job)
        sent_back(block(ga, i), rk_s, i, job)
        sent_back(c3_part(i, job), rc_s, i, job)
        for dst, sem in ((fqa, rq_r), (fkv, rk_r), (fc3, rc_r)):
            pltpu.make_async_copy(dst.at[i], dst.at[i], sem.at[i]).wait()

    both_jobs(finish)


def unpack(qa, kv, c3, oa, oq, ok, ov):
    low = lax.broadcasted_iota(jnp.int32, (B, B), 1) < HD

    def pair(even, odd, first, last):
        first[...] = jnp.where(low, even, pltpu.roll(odd, HD, 1))
        last[...] = jnp.where(low, pltpu.roll(even, HD, 1), odd)

    def whole(h):
        above = jnp.broadcast_to(c3[h][:, None, :] * 0.125, (16, 8, B)).reshape(B, B)
        return kv[h] + above

    pair(qa[0], qa[1], oq, oa)
    pair(whole(0), whole(1), ok, ov)


def on_device(queries, keys, values, cotangent):
    hbm = pl.BlockSpec(memory_space=pl.ANY)
    dma = pltpu.SemaphoreType.DMA
    scratch = [pltpu.VMEM(queries.shape, F32)] * 4
    scratch += [
        pltpu.VMEM((12, B, B), F32),
        pltpu.VMEM((12, B, B), F32),
        pltpu.VMEM((SETS * B, B), F32),
        pltpu.VMEM((12 * B, B), F32),
        pltpu.VMEM((B, B), F32),
    ]
    scratch += [pltpu.VMEM((2, B >> m, B), F32) for m in range(5)]
    scratch += [
        pltpu.VMEM((5, 2, B, B), F32),
        pltpu.VMEM((SETS, B, 3 * B), BF16),
        pltpu.VMEM((SETS, 2 * B, B), BF16),
        pltpu.VMEM((9 * B, 3 * B), BF16),
        pltpu.VMEM((2 * B, 9 * B), BF16),
        pltpu.VMEM((9 * B, 2 * B), F32),
        pltpu.VMEM((9 * B, 2 * B), F32),
    ]
    scratch += [pltpu.VMEM((9 * B, 2 * B), BF16)] * 4
    scratch += [
        pltpu.VMEM((SETS * B, B), F32),
        pltpu.VMEM((6 * B, B), F32),
        pltpu.VMEM((5, 2, B, B), F32),
        pltpu.VMEM((5, 2, B, B), F32),
    ]
    scratch += [pltpu.VMEM((2, B >> m, B), F32) for m in range(5)]
    scratch += [
        pltpu.VMEM((12 * B, B), F32),
    ]
    scratch += [dma((4,))] + [dma((12,))] * 4 + [dma] * 2 + [dma((5,))] * 2 + [dma] * 2 + [dma((5,))] * 2
    scratch += [dma((12,))] * 6
    packed = pl.pallas_call(
        kernel,
        out_shape=[jax.ShapeDtypeStruct((12, n, B), F32) for n in (B, B, 16)],
        in_specs=[hbm] * 4,
        out_specs=[hbm] * 3,
        scratch_shapes=scratch,
        compiler_params=pltpu.CompilerParams(
            collective_id=0, has_side_effects=True, vmem_limit_bytes=56 * 2**20
        ),
    )(queries, keys, values, cotangent)
    return pl.pallas_call(
        unpack,
        grid=(HEADS // 2,),
        out_shape=[jax.ShapeDtypeStruct(queries.shape, F32)] * 4,
        in_specs=[pl.BlockSpec((2, n, B), lambda i: (i, 0, 0)) for n in (B, B, 16)],
        out_specs=[pl.BlockSpec((B, B), lambda i: (0, i))] * 4,
    )(*packed)


def solution(mesh):
    spec = P(("seqhi", "seqlo"), None)
    return jax.shard_map(
        on_device, mesh=mesh, in_specs=(spec,) * 4, out_specs=(spec,) * 4, check_vma=False
    )
```

time: 125 us -> 104 us (0.83)
  the two profiles are of different devices: /device:TPU:9 before, /device:TPU:6 now
where the time goes in v2:
time: 104 us
  Pallas kernels  103 us (99%)
    pallas_call x1, Pallas kernels, on_device(): pl.pallas_call(kernel, out_shape=[jax.ShapeDtypeStruct((12, n, B), F32) f...  98.1 us
    pallas_call x1, Pallas kernels, on_device(): pl.pallas_call(unpack, grid=(HEADS // 2,), out_shape=[jax.ShapeDtypeStruc...  4.79 us

profile of v2, /device:TPU:6, one launch (start us, length us, event | category | flops | bytes accessed | tf_op | source)
XLA Modules:
  0.0 103.5 jit_solution(2212058525255140864)
XLA Ops:
  0.6 98.1 %shard_map.75 = (f32[12,128,128]{2,1,0:T(8,128)}, f32[12,128,128]{2,1,0:T(8,128)}, f32[12,16,128]{2,1,0:T(8,128)}) custom-call(f32[128,768]{1,0:T(8,128)} %q_hbm.1, f32[128,768]{1,0:T(8,128)} %k_hbm.1, f32[128,768]{1,0:T(8,128)} %v_hbm.1, f32[128,768]{1,0:T(8,128)} %g_hbm.1), custom_call_target="tpu_custom_call" | custom-call | tf_op jit(solution)/shard_map/pallas_call | solution.py:466
  98.7 4.8 %shard_map.76 = (f32[128,768]{1,0:T(8,128)}, f32[128,768]{1,0:T(8,128)}, f32[128,768]{1,0:T(8,128)}, f32[128,768]{1,0:T(8,128)}) custom-call(f32[12,128,128]{2,1,0:T(8,128)} %get-tuple-element.7.qa, f32[12,128,128]{2,1,0:T(8,128)} %get-tuple-element.8.kv, f32[12,16,128]{2,1,0:T(8,128)} %get-tuple-element.9.c3), custom_call_target="tpu_custom_call" | custom-call | tf_op jit(solution)/shard_map/pallas_call | solution.py:476

commit v3 on v2

--- a/solution.py
+++ b/solution.py
@@ -45,16 +45,28 @@
     hi_id, lo_id = lax.axis_index("seqhi"), lax.axis_index("seqlo")
     x, k = lax.div(hi_id, 2), lax.rem(hi_id, 2)
     y, z = lax.div(lo_id, 8), lax.rem(lo_id, 8)
+    t = lax.div(z, 2)
     cw = lax.rem(z, 2)
-    t = lax.div(z, 2)
     quad = lax.div(z, 4)
-    p = x * 8 + cw * 4 + y
+    p = (x * 8 + k * 4 + y, x * 8 + cw * 4 + y)
     other = (x * 2 + 1 - k, lo_id)
-    here = cw == k
-
-    def subtree_device(pp):
+
+    def subtree_device(pp, job):
         xx, rest = lax.div(pp, 8), lax.rem(pp, 8)
-        return (xx * 2 + k, lax.rem(rest, 4) * 8 + 2 * t + lax.div(rest, 4))
+        cc, yy = lax.div(rest, 4), lax.rem(rest, 4)
+        if job == 0:
+            return (xx * 2 + cc, yy * 8 + z)
+        return (xx * 2 + k, yy * 8 + 2 * t + cc)
+
+    def worker(u, j, shared):
+        if shared:
+            return quad, 2 * u + k
+        return k, 2 * u + lax.div(j, 2)
+
+    def owner(slot, job):
+        if job == 0:
+            return k, slot, 3 * t + 2 * cw
+        return cw, 4 * k + slot - OWN_B, 3 * t + 1
 
     loads = [
         pltpu.make_async_copy(src, dst, in_s.at[i])
@@ -68,25 +80,32 @@
     def greet(dev):
         pl.semaphore_signal(barrier, inc=1, device_id=dev, device_id_type=MESH)
 
+    def greet_unless_me(core, zz):
+        @pl.when(jnp.logical_not((core == k) & (zz == z)))
+        def _():
+            greet((x * 2 + core, y * 8 + zz))
+
     def greet_ring(i, _):
-        @pl.when(jnp.logical_not(here & (i == z)))
-        def _():
-            greet((x * 2 + cw, y * 8 + i))
-        wk, wz = lax.rem(i, 2), 2 * lax.div(i, 2) + k
-
-        @pl.when(jnp.logical_not((wk == k) & (wz == z)))
-        def _():
-            greet((x * 2 + wk, y * 8 + wz))
+        greet_unless_me(k, i)
         return 0
 
+    def greet_shared(i, _):
+        greet_unless_me(*worker(i, 1, True))
+        greet_unless_me(*owner(OWN_B + i, 1)[:2])
+        return 0
+
+    def greet_sub(i, _):
+        greet(subtree_device(lax.rem(p[0] + i, 32), 0))
+        return 0
+
+    def greet_turned(i, _):
+        greet(subtree_device(lax.div(i, 4) * 8 + (1 - cw) * 4 + lax.rem(i, 4), 1))
+        return 0
+
     lax.fori_loop(0, 8, greet_ring, 0)
-    greet(other)
-
-    def greet_sub(i, _):
-        greet(subtree_device(lax.rem(p + i, 32)))
-        return 0
-
+    lax.fori_loop(0, 4, greet_shared, 0)
     lax.fori_loop(1, 32, greet_sub, 0)
+    lax.fori_loop(0, 16, greet_turned, 0)
 
     low = lax.broadcasted_iota(jnp.int32, (B, B), 1) < HD
 
@@ -102,38 +121,57 @@
     loads[0].wait()
     loads[1].wait()
     pack(k_ref, v_ref, kvs, 1.0)
-    pl.semaphore_wait(barrier, 48 - 2 * (1 - lax.rem(cw + k, 2)))
-
-    def send_out(src, dst, ssem, rsem, heads):
+    pl.semaphore_wait(barrier, 62 - 2 * (1 - lax.rem(cw + k, 2)) * (1 - lax.rem(quad + k, 2)))
+
+    def turn(i, n):
+        return lax.rem(i + k * (n - 2 * i) + n, n)
+
+    def send_head(src, dst, ssem, rsem, u, j, shared=False):
+        h = 3 * u + j
+        wk, wz = worker(u, j, shared)
+        slot = 8 + lax.rem(z, 4) if shared else z
+        me = (wz == z) & (wk == k)
+
+        @pl.when(me)
+        def _():
+            pltpu.make_async_copy(src.at[h], dst.at[rows(slot * B, B)], rsem.at[slot]).start()
+
+        @pl.when(jnp.logical_not(me))
+        def _():
+            pltpu.make_async_remote_copy(
+                src.at[h], dst.at[rows(slot * B, B)], ssem.at[h], rsem.at[slot],
+                device_id=(x * 2 + wk, y * 8 + wz), device_id_type=MESH,
+            ).start()
+
+    def send_shared(src, dst, ssem, rsem):
         def step(i, _):
-            u = lax.rem(i + t, 4)
-            wz = 2 * u + k
-            for j in heads:
-                h = 3 * u + j
-                wk = (0, quad, 1)[j]
-                slot = z if j != 1 else 8 + lax.rem(z, 4)
-                me = (wz == z) & (wk == k)
-
-                @pl.when(me)
-                def _():
-                    pltpu.make_async_copy(src.at[h], dst.at[rows(slot * B, B)], rsem.at[slot]).start()
-
-                @pl.when(jnp.logical_not(me))
-                def _():
-                    pltpu.make_async_remote_copy(
-                        src.at[h], dst.at[rows(slot * B, B)], ssem.at[h], rsem.at[slot],
-                        device_id=(x * 2 + wk, y * 8 + wz), device_id_type=MESH,
-                    ).start()
+            send_head(src, dst, ssem, rsem, lax.rem(t + turn(i, 4), 4), 1, True)
             return 0
 
         lax.fori_loop(0, 4, step, 0)
+
+    def send_own(src, dst, ssem, rsem):
+        def step(i, _):
+            u = lax.rem(t + turn(i, 4), 4)
+            for j in (0, 2):
+                send_head(src, dst, ssem, rsem, u, j)
+            return 0
+
+        lax.fori_loop(0, 4, step, 0)
+
+    def send_own_far(src, dst, ssem, rsem):
+        def step(i, _):
+            wz = lax.rem(z + turn(lax.rem(4 + i, 8), 8), 8)
+            send_head(src, dst, ssem, rsem, lax.div(wz, 2), 2 * lax.rem(wz, 2))
+            return 0
+
+        lax.fori_loop(0, 8, step, 0)
 
     def sent_out(src, ssem):
         def step(u, _):
-            wz = 2 * u + k
             for j in range(3):
                 h = 3 * u + j
-                wk = (0, quad, 1)[j]
+                wk, wz = worker(u, j, j == 1)
 
                 @pl.when(jnp.logical_not((wz == z) & (wk == k)))
                 def _():
@@ -146,14 +184,9 @@
         part = dst.at[rows(slot * B, B)]
         pltpu.make_async_copy(part, part, rsem.at[slot]).wait()
 
-    def owner(slot, job):
-        if job == 0:
-            return slot, 3 * t + 2 * k
-        return 4 * k + slot - OWN_B, 3 * t + 1
-
     def send_back(part, dst, ssem, rsem, slot, job):
-        oz, h = owner(slot, job)
-        me = here & (oz == z)
+        oc, oz, h = owner(slot, job)
+        me = (oc == k) & (oz == z)
 
         @pl.when(me)
         def _():
@@ -163,13 +196,13 @@
         def _():
             pltpu.make_async_remote_copy(
                 part, dst.at[h], ssem.at[slot], rsem.at[h],
-                device_id=(x * 2 + cw, y * 8 + oz), device_id_type=MESH,
+                device_id=(x * 2 + oc, y * 8 + oz), device_id_type=MESH,
             ).start()
 
     def sent_back(part, ssem, slot, job):
-        oz, _ = owner(slot, job)
-
-        @pl.when(jnp.logical_not(here & (oz == z)))
+        oc, oz, _ = owner(slot, job)
+
+        @pl.when(jnp.logical_not((oc == k) & (oz == z)))
         def _():
             pltpu.make_async_copy(part, part, ssem.at[slot]).wait()
 
@@ -177,7 +210,19 @@
         return ref.at[rows(slot * B, B)]
 
     def c3_part(slot, job):
-        return u3.at[job, rows(16 * owner(slot, job)[0], 16), :]
+        return u3.at[job, rows(16 * owner(slot, job)[1], 16), :]
+
+    def both_jobs_round(what):
+        def shared(i, _):
+            what(8 + lax.rem(z + i, 4), 1)
+            return 0
+
+        def own(i, _):
+            what(lax.rem(z + turn(lax.rem(4 + i, 8), 8), 8), 0)
+            return 0
+
+        lax.fori_loop(0, 4, shared, 0)
+        lax.fori_loop(0, 8, own, 0)
 
     def both_jobs(what):
         for job, (first, last) in enumerate(((0, 8), (8, 12))):
@@ -190,31 +235,33 @@
     def send_subtrees(m, src_part, dst, ssem, rsem):
         size = 2**m
         n = B // size
-        group = lax.div(p, size)
-        base = (group + 1 - 2 * lax.rem(group, 2)) * size
-        mine = lax.rem(p, size) * n
-
-        def step(i, _):
-            j = lax.rem(i + p, size)
-            pltpu.make_async_remote_copy(
-                src_part(j, n), dst.at[m, :, rows(mine, n), :], ssem.at[m], rsem.at[m],
-                device_id=subtree_device(base + j), device_id_type=MESH,
-            ).start()
-            return 0
-
-        lax.fori_loop(0, size, step, 0)
+        for job in range(2):
+            group = lax.div(p[job], size)
+            base = (group + 1 - 2 * lax.rem(group, 2)) * size
+            mine = lax.rem(p[job], size) * n
+
+            def step(i, _, job=job, base=base, mine=mine):
+                j = lax.rem(i + p[job], size)
+                pltpu.make_async_remote_copy(
+                    src_part(job, j, n), dst.at[m, job, rows(mine, n), :], ssem.at[m], rsem.at[m],
+                    device_id=subtree_device(base + j, job), device_id_type=MESH,
+                ).start()
+                return 0
+
+            lax.fori_loop(0, size, step, 0)
 
     def wait_all(ref, sem):
         pltpu.make_async_copy(ref, ref, sem).wait()
 
-    send_out(kvs, kvr, kv_s, kv_r, (1, 0, 2))
+    send_shared(kvs, kvr, kv_s, kv_r)
+    send_own_far(kvs, kvr, kv_s, kv_r)
     loads[2].wait()
     loads[3].wait()
     pack(q_ref, g_ref, qgs, 0.125)
     for start, count in ((C2_A, SETS - C2_A),):
         ga[start * B : (start + count) * B] = jnp.zeros((count * B, B), F32)
     sent_out(kvs, kv_s)
-    send_out(qgs, qgr, qg_s, qg_r, (1,))
+    send_shared(qgs, qgr, qg_s, qg_r)
 
     def put(index, v):
         h = v.astype(BF16)
@@ -254,8 +301,8 @@
         if m:
             for job in range(2):
                 levels[m][job] = halve(levels[m - 1].at[job], 0, B >> m)
-        send_subtrees(m, lambda j, n: levels[m], sib, sb_s, sb_r)
-    send_out(qgs, qgr, qg_s, qg_r, (0, 2))
+        send_subtrees(m, lambda job, j, n: levels[m].at[job], sib, sb_s, sb_r)
+    send_own(qgs, qgr, qg_s, qg_r)
 
     def put_step(i, _):
         put(i, kvr[rows(i * B, B), :])
@@ -353,7 +400,7 @@
             load_set(4 + m, (SIB_A, SIB_B)[job] + m)
 
         def step(i, _):
-            run_pair(i if job else lax.rem(t + 4 - i, 4), job)
+            run_pair(i if job else lax.rem(t + 4 - turn(i, 4), 4), job)
             return 0
 
         lax.fori_loop(0, count, step, 0)
@@ -373,7 +420,7 @@
     for m in range(5):
         gs[m, 0] = ga[(SIB_A + m) * B : (SIB_A + m + 1) * B]
         gs[m, 1] = ga[(SIB_B + m) * B : (SIB_B + m + 1) * B] + xr[(1 + m) * B : (2 + m) * B]
-        send_subtrees(m, lambda j, n: gs.at[m, :, rows(j * n, n), :], gr, gs_s, gs_r)
+        send_subtrees(m, lambda job, j, n: gs.at[m, job, rows(j * n, n), :], gr, gs_s, gs_r)
 
     for i in range(2):
         spread(ga[(C2_A + i) * B : (C2_A + i + 1) * B], ga, (C1_A + 2 * i) * B, B)
@@ -382,7 +429,7 @@
     spread(xr[0:B], ga, C1_B * B, B)
     for i in range(2):
         spread(ga[(C1_B + i) * B : (C1_B + i + 1) * B], ga, (OWN_B + 2 * i) * B, B)
-    both_jobs(lambda i, job: send_back(block(ga, i), fkv, rk_s, rk_r, i, job))
+    both_jobs_round(lambda i, job: send_back(block(ga, i), fkv, rk_s, rk_r, i, job))
 
     ups = (u3, u4, u5, u6, u7)
     for m in (4, 3, 2, 1, 0):
@@ -396,7 +443,7 @@
     for m in (4, 3, 2, 1):
         for job in range(2):
             spread(ups[m][job], ups[m - 1].at[job], 0, B >> m)
-    both_jobs(lambda i, job: send_back(c3_part(i, job), fc3, rc_s, rc_r, i, job))
+    both_jobs_round(lambda i, job: send_back(c3_part(i, job), fc3, rc_s, rc_r, i, job))
 
     sent_out(qgs, qg_s)
     cx.wait_send()
@@ -425,8 +472,10 @@
         above = jnp.broadcast_to(c3[h][:, None, :] * 0.125, (16, 8, B)).reshape(B, B)
         return kv[h] + above
 
-    pair(qa[0], qa[1], oq, oa)
-    pair(whole(0), whole(1), ok, ov)
+    for i in range(3):
+        cols = slice(i * B, (i + 1) * B)
+        pair(qa[2 * i], qa[2 * i + 1], oq.at[:, cols], oa.at[:, cols])
+        pair(whole(2 * i), whole(2 * i + 1), ok.at[:, cols], ov.at[:, cols])
 
 
 def on_device(queries, keys, values, cotangent):
@@ -475,10 +524,10 @@
     )(queries, keys, values, cotangent)
     return pl.pallas_call(
         unpack,
-        grid=(HEADS // 2,),
+        grid=(HEADS // 6,),
         out_shape=[jax.ShapeDtypeStruct(queries.shape, F32)] * 4,
-        in_specs=[pl.BlockSpec((2, n, B), lambda i: (i, 0, 0)) for n in (B, B, 16)],
-        out_specs=[pl.BlockSpec((B, B), lambda i: (0, i))] * 4,
+        in_specs=[pl.BlockSpec((6, n, B), lambda i: (i, 0, 0)) for n in (B, B, 16)],
+        out_specs=[pl.BlockSpec((B, 3 * B), lambda i: (0, i))] * 4,
     )(*packed)
 
 

time: 104 us -> 93.9 us (0.903)
  Pallas kernels: 103 us -> 92.4 us
    pallas_call x1, Pallas kernels: 98.1 us -> 89.9 us  [on_device(): pl.pallas_call(kernel, out_shape=[jax.ShapeDtypeStruct((12, n, B), F32) f...]
    pallas_call x1, Pallas kernels: 4.79 us -> 2.52 us  [on_device(): pl.pallas_call(unpack, grid=(HEADS // 6,), out_shape=[jax.ShapeDtypeStruc...]
where the time goes in v3:
time: 93.9 us; the launch traced here: 93 us
  Pallas kernels  92.4 us (98%)
    pallas_call x1, Pallas kernels, on_device(): pl.pallas_call(kernel, out_shape=[jax.ShapeDtypeStruct((12, n, B), F32) f...  89.9 us
    pallas_call x1, Pallas kernels, on_device(): pl.pallas_call(unpack, grid=(HEADS // 6,), out_shape=[jax.ShapeDtypeStruc...  2.52 us

profile of v3, /device:TPU:6, one launch (start us, length us, event | category | flops | bytes accessed | tf_op | source)
XLA Modules:
  0.0 93.0 jit_solution(7430385777791940989)
XLA Ops:
  0.6 89.9 %shard_map.75 = (f32[12,128,128]{2,1,0:T(8,128)}, f32[12,128,128]{2,1,0:T(8,128)}, f32[12,16,128]{2,1,0:T(8,128)}) custom-call(f32[128,768]{1,0:T(8,128)} %q_hbm.1, f32[128,768]{1,0:T(8,128)} %k_hbm.1, f32[128,768]{1,0:T(8,128)} %v_hbm.1, f32[128,768]{1,0:T(8,128)} %g_hbm.1), custom_call_target="tpu_custom_call" | custom-call | tf_op jit(solution)/shard_map/pallas_call | solution.py:515
  90.5 2.5 %shard_map.76 = (f32[128,768]{1,0:T(8,128)}, f32[128,768]{1,0:T(8,128)}, f32[128,768]{1,0:T(8,128)}, f32[128,768]{1,0:T(8,128)}) custom-call(f32[12,128,128]{2,1,0:T(8,128)} %get-tuple-element.7.qa, f32[12,128,128]{2,1,0:T(8,128)} %get-tuple-element.8.kv, f32[12,16,128]{2,1,0:T(8,128)} %get-tuple-element.9.c3), custom_call_target="tpu_custom_call" | custom-call | tf_op jit(solution)/shard_map/pallas_call | solution.py:525

commit v4 on v3

--- a/solution.py
+++ b/solution.py
@@ -16,6 +16,8 @@
 B = 128
 LOG_TWO = math.log(2.0)
 NT = (((1,), (1,)), ((), ()))
+NEAR = (0, 1, 7, 2, 6, 3, 5, 4)
+LATE = (6, 3, 5, 4)
 
 OWN_A, OWN_B, C1_A, C1_B, C2_A, SIB_A, C2_O, SIB_B, SETS = 0, 8, 12, 16, 18, 20, 25, 26, 31
 
@@ -38,7 +40,7 @@
     fqa, fkv, fc3,
     q_ref, k_ref, v_ref, g_ref,
     kvs, qgs, kvr, qgr, c2o, cs3, cs4, cs5, cs6, cs7, sib,
-    hl, hlt, xs, xt, sd, dp, ph, plo, dh, dl, ga, xr, gs, gr, u3, u4, u5, u6, u7, rqa,
+    hl, hlt, xs, xt, sd, dp, ph, plo, dh, dl, ga, xr, gs, gr, u3, u4, u5, u6, u7, nought, rqa,
     in_s, kv_s, kv_r, qg_s, qg_r, cx_s, cx_r, sb_s, sb_r, gx_s, gx_r, gs_s, gs_r,
     rq_s, rq_r, rk_s, rk_r, rc_s, rc_r,
 ):
@@ -48,15 +50,19 @@
     t = lax.div(z, 2)
     cw = lax.rem(z, 2)
     quad = lax.div(z, 4)
-    p = (x * 8 + k * 4 + y, x * 8 + cw * 4 + y)
+    core_of = (k, cw)
     other = (x * 2 + 1 - k, lo_id)
 
-    def subtree_device(pp, job):
-        xx, rest = lax.div(pp, 8), lax.rem(pp, 8)
-        cc, yy = lax.div(rest, 4), lax.rem(rest, 4)
+    def flip(i):
+        return i + 1 - 2 * lax.rem(i, 2)
+
+    flip_z, flip_x, flip_y = flip(z), flip(x), flip(y)
+    far_x, far_y = 2 * (1 - lax.div(x, 2)), 2 * (1 - lax.div(y, 2))
+
+    def place(job, xx, turn, yy):
         if job == 0:
-            return (xx * 2 + cc, yy * 8 + z)
-        return (xx * 2 + k, yy * 8 + 2 * t + cc)
+            return (xx * 2 + (1 - k if turn else k), yy * 8 + z)
+        return (xx * 2 + k, yy * 8 + (flip_z if turn else z))
 
     def worker(u, j, shared):
         if shared:
@@ -94,18 +100,16 @@
         greet_unless_me(*owner(OWN_B + i, 1)[:2])
         return 0
 
-    def greet_sub(i, _):
-        greet(subtree_device(lax.rem(p[0] + i, 32), 0))
-        return 0
-
-    def greet_turned(i, _):
-        greet(subtree_device(lax.div(i, 4) * 8 + (1 - cw) * 4 + lax.rem(i, 4), 1))
-        return 0
-
     lax.fori_loop(0, 8, greet_ring, 0)
     lax.fori_loop(0, 4, greet_shared, 0)
-    lax.fori_loop(1, 32, greet_sub, 0)
-    lax.fori_loop(0, 16, greet_turned, 0)
+    for xx in range(4):
+        for yy in range(4):
+            greet(place(0, xx, True, yy))
+            greet(place(1, xx, True, yy))
+
+            @pl.when(jnp.logical_not((xx == x) & (yy == y)))
+            def _():
+                greet(place(0, xx, False, yy))
 
     low = lax.broadcasted_iota(jnp.int32, (B, B), 1) < HD
 
@@ -159,13 +163,10 @@
 
         lax.fori_loop(0, 4, step, 0)
 
-    def send_own_far(src, dst, ssem, rsem):
-        def step(i, _):
-            wz = lax.rem(z + turn(lax.rem(4 + i, 8), 8), 8)
+    def send_own_near(src, dst, ssem, rsem):
+        for d in NEAR:
+            wz = lax.rem(z + d, 8)
             send_head(src, dst, ssem, rsem, lax.div(wz, 2), 2 * lax.rem(wz, 2))
-            return 0
-
-        lax.fori_loop(0, 8, step, 0)
 
     def sent_out(src, ssem):
         def step(u, _):
@@ -190,12 +191,12 @@
 
         @pl.when(me)
         def _():
-            pltpu.make_async_copy(part, dst.at[h], rsem.at[h]).start()
+            pltpu.make_async_copy(part, dst.at[h], rsem).start()
 
         @pl.when(jnp.logical_not(me))
         def _():
             pltpu.make_async_remote_copy(
-                part, dst.at[h], ssem.at[slot], rsem.at[h],
+                part, dst.at[h], ssem.at[slot], rsem,
                 device_id=(x * 2 + oc, y * 8 + oz), device_id_type=MESH,
             ).start()
 
@@ -212,17 +213,15 @@
     def c3_part(slot, job):
         return u3.at[job, rows(16 * owner(slot, job)[1], 16), :]
 
-    def both_jobs_round(what):
+    def round_early(what):
         def shared(i, _):
             what(8 + lax.rem(z + i, 4), 1)
             return 0
 
-        def own(i, _):
-            what(lax.rem(z + turn(lax.rem(4 + i, 8), 8), 8), 0)
-            return 0
-
         lax.fori_loop(0, 4, shared, 0)
-        lax.fori_loop(0, 8, own, 0)
+        for d in NEAR:
+            if d not in LATE:
+                what(lax.rem(z + d, 8), 0)
 
     def both_jobs(what):
         for job, (first, last) in enumerate(((0, 8), (8, 12))):
@@ -232,29 +231,43 @@
 
             lax.fori_loop(first, last, step, 0)
 
-    def send_subtrees(m, src_part, dst, ssem, rsem):
-        size = 2**m
-        n = B // size
+    def sibling(m, turned):
+        if m == 0:
+            return [(0, x, False, flip_y)]
+        if m == 1:
+            return [(e, x, False, far_y + e) for e in range(2)]
+        if m == 2:
+            return [(yy, x, True, yy) for yy in range(4)]
+        out = []
+        for e in range(m - 2):
+            for first in range(2):
+                xx = flip_x if m == 3 else far_x + e
+                out += [(e * 8 + 4 * first + yy, xx, first, yy) for yy in range(4)]
+        return out
+
+    def send_subtrees(m, src_part, dst, ssem, rsem, halved=False):
+        n = B >> m
         for job in range(2):
-            group = lax.div(p[job], size)
-            base = (group + 1 - 2 * lax.rem(group, 2)) * size
-            mine = lax.rem(p[job], size) * n
-
-            def step(i, _, job=job, base=base, mine=mine):
-                j = lax.rem(i + p[job], size)
+            c = core_of[job]
+            own = m + 5 * job if halved else m
+            mine = lax.rem((x * 8 + c * 4 + y), 2**m) * n
+            for j, xx, turned, yy in sibling(m, c):
+                if m >= 3:
+                    index = (j // 8) * 8 + lax.rem(c + (j // 4) % 2, 2) * 4 + j % 4
+                else:
+                    index = j
+                at, count = (k * (n // 2), n // 2) if halved and job == 1 and m < 4 else (0, n)
                 pltpu.make_async_remote_copy(
-                    src_part(job, j, n), dst.at[m, job, rows(mine, n), :], ssem.at[m], rsem.at[m],
-                    device_id=subtree_device(base + j, job), device_id_type=MESH,
+                    src_part(job, index * n + at, count), dst.at[m, job, rows(mine + at, count), :],
+                    ssem.at[own], rsem.at[own],
+                    device_id=place(job, xx, turned, yy), device_id_type=MESH,
                 ).start()
-                return 0
-
-            lax.fori_loop(0, size, step, 0)
 
     def wait_all(ref, sem):
         pltpu.make_async_copy(ref, ref, sem).wait()
 
     send_shared(kvs, kvr, kv_s, kv_r)
-    send_own_far(kvs, kvr, kv_s, kv_r)
+    send_own_near(kvs, kvr, kv_s, kv_r)
     loads[2].wait()
     loads[3].wait()
     pack(q_ref, g_ref, qgs, 0.125)
@@ -301,7 +314,7 @@
         if m:
             for job in range(2):
                 levels[m][job] = halve(levels[m - 1].at[job], 0, B >> m)
-        send_subtrees(m, lambda job, j, n: levels[m].at[job], sib, sb_s, sb_r)
+        send_subtrees(m, lambda job, at, n: levels[m].at[job], sib, sb_s, sb_r)
     send_own(qgs, qgr, qg_s, qg_r)
 
     def put_step(i, _):
@@ -312,21 +325,12 @@
     put(C2_O, c2o[...])
     for m in range(5):
         wait_all(sib.at[m], sb_r.at[m])
-
-    def put_sib(m, _):
-        put(SIB_A + m, sib[m, 0])
         put(SIB_B + m, sib[m, 1])
-        return 0
-
-    lax.fori_loop(0, 5, put_sib, 0)
 
     def load_set(position, index):
         part = slice(position * B, (position + 1) * B)
         xs[part, :] = hl[index]
         xt[:, part] = hlt[index]
-
-    def flip(i):
-        return i + 1 - 2 * lax.rem(i, 2)
 
     low2 = lax.broadcasted_iota(jnp.int32, (2 * B, B), 1) < HD
 
@@ -397,6 +401,8 @@
 
     def run_job(job, count):
         for m in range(5):
+            if job == 0:
+                put(SIB_A + m, sib[m, 0])
             load_set(4 + m, (SIB_A, SIB_B)[job] + m)
 
         def step(i, _):
@@ -420,7 +426,7 @@
     for m in range(5):
         gs[m, 0] = ga[(SIB_A + m) * B : (SIB_A + m + 1) * B]
         gs[m, 1] = ga[(SIB_B + m) * B : (SIB_B + m + 1) * B] + xr[(1 + m) * B : (2 + m) * B]
-        send_subtrees(m, lambda job, j, n: gs.at[m, job, rows(j * n, n), :], gr, gs_s, gs_r)
+        send_subtrees(m, lambda job, at, n: gs.at[m, job, rows(at, n), :], gr, gs_s, gs_r, True)
 
     for i in range(2):
         spread(ga[(C2_A + i) * B : (C2_A + i + 1) * B], ga, (C1_A + 2 * i) * B, B)
@@ -429,36 +435,70 @@
     spread(xr[0:B], ga, C1_B * B, B)
     for i in range(2):
         spread(ga[(C1_B + i) * B : (C1_B + i + 1) * B], ga, (OWN_B + 2 * i) * B, B)
-    both_jobs_round(lambda i, job: send_back(block(ga, i), fkv, rk_s, rk_r, i, job))
+    def send_now(i, job):
+        send_back(block(ga, i), fkv, rk_s, rk_r, i, job)
+
+    round_early(send_now)
+
+    nought[...] = jnp.zeros_like(nought)
+    for d in LATE:
+        wz = lax.rem(z + 8 - d, 8)
+        pltpu.make_async_copy(nought, fc3.at[3 * lax.div(wz, 2) + 2 * lax.rem(wz, 2)], rc_r).start()
+
+
+    def wait_halved(m, sem):
+        wait_all(gr.at[m, 0], sem.at[m])
+        wait_all(gr.at[m, 1] if m == 4 else gr.at[m, 1, 0:64], sem.at[5 + m])
 
     ups = (u3, u4, u5, u6, u7)
     for m in (4, 3, 2, 1, 0):
-        wait_all(gr.at[m], gs_r.at[m])
+        wait_halved(m, gs_r)
         n = B >> m
-        for job in range(2):
-            acc = gr[m, job, 0:n]
-            for j in range(1, 2**m):
-                acc = acc + gr[m, job, j * n : (j + 1) * n]
-            ups[m][job] = acc
+        acc = gr[m, 0, 0:n]
+        for j in range(1, 2**m):
+            acc = acc + gr[m, 0, j * n : (j + 1) * n]
+        ups[m][0] = acc
+        at, count = (k * (n // 2), n // 2) if m < 4 else (0, n)
+        acc = gr[m, 1, rows(at, count), :]
+        for j in range(1, 2**m):
+            acc = acc + gr[m, 1, rows(j * n + at, count), :]
+        if m == 3:
+            u6[1] = jnp.zeros((16, B), F32)
+        ups[m][1, rows(at, count), :] = acc
     for m in (4, 3, 2, 1):
-        for job in range(2):
-            spread(ups[m][job], ups[m - 1].at[job], 0, B >> m)
-    both_jobs_round(lambda i, job: send_back(c3_part(i, job), fc3, rc_s, rc_r, i, job))
+        n = B >> m
+        spread(ups[m][0], ups[m - 1].at[0], 0, n)
+        if m == 4:
+            spread(u7[1], u6.at[1], 0, n)
+        else:
+            h = n // 2
+            spread(ups[m][1, rows(k * h, h), :], ups[m - 1].at[1], 2 * k * h, h)
+
+    def send_late(i, job):
+        above = u3[job, rows(16 * owner(i, job)[1], 16), :] * 0.125
+        part = rows(i * B, B)
+        ga[part, :] = ga[part, :] + jnp.broadcast_to(above[:, None, :], (16, 8, B)).reshape(B, B)
+        send_now(i, job)
+
+    for d in LATE:
+        send_late(lax.rem(z + d, 8), 0)
+    round_early(lambda i, job: send_back(c3_part(i, job), fc3, rc_s, rc_r, i, job))
 
     sent_out(qgs, qg_s)
     cx.wait_send()
     for m in range(5):
         wait_all(sib.at[m], sb_s.at[m])
-        wait_all(gr.at[m], gs_s.at[m])
+        wait_halved(m, gs_s)
+    both_jobs(lambda i, job: sent_back(block(rqa, i), rq_s, i, job))
+    wait_all(fqa, rq_r)
 
     def finish(i, job):
-        sent_back(block(rqa, i), rq_s, i, job)
         sent_back(block(ga, i), rk_s, i, job)
-        sent_back(c3_part(i, job), rc_s, i, job)
-        for dst, sem in ((fqa, rq_r), (fkv, rk_r), (fc3, rc_r)):
-            pltpu.make_async_copy(dst.at[i], dst.at[i], sem.at[i]).wait()
 
     both_jobs(finish)
+    round_early(lambda i, job: sent_back(c3_part(i, job), rc_s, i, job))
+    wait_all(fkv, rk_r)
+    wait_all(fc3, rc_r)
 
 
 def unpack(qa, kv, c3, oa, oq, ok, ov):
@@ -508,10 +548,11 @@
     ]
     scratch += [pltpu.VMEM((2, B >> m, B), F32) for m in range(5)]
     scratch += [
+        pltpu.VMEM((16, B), F32),
         pltpu.VMEM((12 * B, B), F32),
     ]
-    scratch += [dma((4,))] + [dma((12,))] * 4 + [dma] * 2 + [dma((5,))] * 2 + [dma] * 2 + [dma((5,))] * 2
-    scratch += [dma((12,))] * 6
+    scratch += [dma((4,))] + [dma((12,))] * 4 + [dma] * 2 + [dma((5,))] * 2 + [dma] * 2 + [dma((10,))] * 2
+    scratch += [dma((12,)), dma] * 3
     packed = pl.pallas_call(
         kernel,
         out_shape=[jax.ShapeDtypeStruct((12, n, B), F32) for n in (B, B, 16)],

time: 93.9 us -> 90.6 us (0.965)
  Pallas kernels: 92.4 us -> 89 us
    pallas_call x1, Pallas kernels: 89.9 us -> 86.5 us  [on_device(): pl.pallas_call(kernel, out_shape=[jax.ShapeDtypeStruct((12, n, B), F32) f...]
where the time goes in v4:
time: 90.6 us; the launch traced here: 89.7 us
  Pallas kernels  89 us (98%)
    pallas_call x1, Pallas kernels, on_device(): pl.pallas_call(kernel, out_shape=[jax.ShapeDtypeStruct((12, n, B), F32) f...  86.5 us
    pallas_call x1, Pallas kernels, on_device(): pl.pallas_call(unpack, grid=(HEADS // 6,), out_shape=[jax.ShapeDtypeStruc...  2.52 us

profile of v4, /device:TPU:6, one launch (start us, length us, event | category | flops | bytes accessed | tf_op | source)
XLA Modules:
  0.0 89.7 jit_solution(16989718326634894022)
XLA Ops:
  0.6 86.5 %shard_map.75 = (f32[12,128,128]{2,1,0:T(8,128)}, f32[12,128,128]{2,1,0:T(8,128)}, f32[12,16,128]{2,1,0:T(8,128)}) custom-call(f32[128,768]{1,0:T(8,128)} %q_hbm.1, f32[128,768]{1,0:T(8,128)} %k_hbm.1, f32[128,768]{1,0:T(8,128)} %v_hbm.1, f32[128,768]{1,0:T(8,128)} %g_hbm.1), custom_call_target="tpu_custom_call" | custom-call | tf_op jit(solution)/shard_map/pallas_call | solution.py:556
  87.1 2.5 %shard_map.76 = (f32[128,768]{1,0:T(8,128)}, f32[128,768]{1,0:T(8,128)}, f32[128,768]{1,0:T(8,128)}, f32[128,768]{1,0:T(8,128)}) custom-call(f32[12,128,128]{2,1,0:T(8,128)} %get-tuple-element.7.qa, f32[12,128,128]{2,1,0:T(8,128)} %get-tuple-element.8.kv, f32[12,16,128]{2,1,0:T(8,128)} %get-tuple-element.9.c3), custom_call_target="tpu_custom_call" | custom-call | tf_op jit(solution)/shard_map/pallas_call | solution.py:566

commit v5 on v4

--- a/solution.py
+++ b/solution.py
@@ -17,7 +17,7 @@
 LOG_TWO = math.log(2.0)
 NT = (((1,), (1,)), ((), ()))
 NEAR = (0, 1, 7, 2, 6, 3, 5, 4)
-LATE = (6, 3, 5, 4)
+LATE = (3, 5, 4)
 
 OWN_A, OWN_B, C1_A, C1_B, C2_A, SIB_A, C2_O, SIB_B, SETS = 0, 8, 12, 16, 18, 20, 25, 26, 31
 
@@ -214,11 +214,6 @@
         return u3.at[job, rows(16 * owner(slot, job)[1], 16), :]
 
     def round_early(what):
-        def shared(i, _):
-            what(8 + lax.rem(z + i, 4), 1)
-            return 0
-
-        lax.fori_loop(0, 4, shared, 0)
         for d in NEAR:
             if d not in LATE:
                 what(lax.rem(z + d, 8), 0)
@@ -297,7 +292,7 @@
         kvr[(C1_B + i) * B : (C1_B + i + 1) * B] = halve(kvr, (OWN_B + 2 * i) * B, B)
     kvr[30 * B : 31 * B] = halve(kvr, C1_B * B, B)
     c2_mine = kvr.at[pl.ds(30 * B, B)]
-    cx = pltpu.make_async_remote_copy(c2_mine, c2o, cx_s, cx_r, device_id=other, device_id_type=MESH)
+    cx = pltpu.make_async_remote_copy(c2_mine, c2o.at[pl.ds(0, B)], cx_s, cx_r, device_id=other, device_id_type=MESH)
     cx.start()
     for s in range(8):
         landed(kvr, kv_r, s)
@@ -322,7 +317,7 @@
         return 0
 
     lax.fori_loop(0, 20, put_step, 0)
-    put(C2_O, c2o[...])
+    put(C2_O, c2o[0:B])
     for m in range(5):
         wait_all(sib.at[m], sb_r.at[m])
         put(SIB_B + m, sib[m, 1])
@@ -441,6 +436,8 @@
     round_early(send_now)
 
     nought[...] = jnp.zeros_like(nought)
+    for u in range(4):
+        pltpu.make_async_copy(nought, fc3.at[3 * u + 1], rc_r).start()
     for d in LATE:
         wz = lax.rem(z + 8 - d, 8)
         pltpu.make_async_copy(nought, fc3.at[3 * lax.div(wz, 2) + 2 * lax.rem(wz, 2)], rc_r).start()
@@ -480,6 +477,11 @@
         ga[part, :] = ga[part, :] + jnp.broadcast_to(above[:, None, :], (16, 8, B)).reshape(B, B)
         send_now(i, job)
 
+    def late_shared(i, _):
+        send_late(8 + lax.rem(z + i, 4), 1)
+        return 0
+
+    lax.fori_loop(0, 4, late_shared, 0)
     for d in LATE:
         send_late(lax.rem(z + d, 8), 0)
     round_early(lambda i, job: send_back(c3_part(i, job), fc3, rc_s, rc_r, i, job))
@@ -525,11 +527,11 @@
     scratch += [
         pltpu.VMEM((12, B, B), F32),
         pltpu.VMEM((12, B, B), F32),
-        pltpu.VMEM((SETS * B, B), F32),
+        pltpu.VMEM(((SETS + 1) * B, B), F32),
         pltpu.VMEM((12 * B, B), F32),
-        pltpu.VMEM((B, B), F32),
+        pltpu.VMEM((2 * B, B), F32),
     ]
-    scratch += [pltpu.VMEM((2, B >> m, B), F32) for m in range(5)]
+    scratch += [pltpu.VMEM((3, B >> m, B), F32) for m in range(5)]
     scratch += [
         pltpu.VMEM((5, 2, B, B), F32),
         pltpu.VMEM((SETS, B, 3 * B), BF16),
@@ -546,7 +548,7 @@
         pltpu.VMEM((5, 2, B, B), F32),
         pltpu.VMEM((5, 2, B, B), F32),
     ]
-    scratch += [pltpu.VMEM((2, B >> m, B), F32) for m in range(5)]
+    scratch += [pltpu.VMEM((3, B >> m, B), F32) for m in range(5)]
     scratch += [
         pltpu.VMEM((16, B), F32),
         pltpu.VMEM((12 * B, B), F32),

time: 90.6 us -> 90.5 us (level)
  no operation moved by 1% of the time
where the time goes in v5:
time: 90.5 us; the launch traced here: 88.8 us
  Pallas kernels  88.1 us (97%)
    pallas_call x1, Pallas kernels, on_device(): pl.pallas_call(kernel, out_shape=[jax.ShapeDtypeStruct((12, n, B), F32) f...  85.6 us
    pallas_call x1, Pallas kernels, on_device(): pl.pallas_call(unpack, grid=(HEADS // 6,), out_shape=[jax.ShapeDtypeStruc...  2.52 us

profile of v5, /device:TPU:6, one launch (start us, length us, event | category | flops | bytes accessed | tf_op | source)
XLA Modules:
  0.0 88.8 jit_solution(14962716310864491929)
XLA Ops:
  0.6 85.6 %shard_map.75 = (f32[12,128,128]{2,1,0:T(8,128)}, f32[12,128,128]{2,1,0:T(8,128)}, f32[12,16,128]{2,1,0:T(8,128)}) custom-call(f32[128,768]{1,0:T(8,128)} %q_hbm.1, f32[128,768]{1,0:T(8,128)} %k_hbm.1, f32[128,768]{1,0:T(8,128)} %v_hbm.1, f32[128,768]{1,0:T(8,128)} %g_hbm.1), custom_call_target="tpu_custom_call" | custom-call | tf_op jit(solution)/shard_map/pallas_call | solution.py:558
  86.2 2.5 %shard_map.76 = (f32[128,768]{1,0:T(8,128)}, f32[128,768]{1,0:T(8,128)}, f32[128,768]{1,0:T(8,128)}, f32[128,768]{1,0:T(8,128)}) custom-call(f32[12,128,128]{2,1,0:T(8,128)} %get-tuple-element.7.qa, f32[12,128,128]{2,1,0:T(8,128)} %get-tuple-element.8.kv, f32[12,16,128]{2,1,0:T(8,128)} %get-tuple-element.9.c3), custom_call_target="tpu_custom_call" | custom-call | tf_op jit(solution)/shard_map/pallas_call | solution.py:568

commit v6 on v5

--- a/solution.py
+++ b/solution.py
@@ -240,9 +240,9 @@
                 out += [(e * 8 + 4 * first + yy, xx, first, yy) for yy in range(4)]
         return out
 
-    def send_subtrees(m, src_part, dst, ssem, rsem, halved=False):
+    def send_subtrees(m, src_part, dst, ssem, rsem, halved=False, jobs=(0, 1)):
         n = B >> m
-        for job in range(2):
+        for job in jobs:
             c = core_of[job]
             own = m + 5 * job if halved else m
             mine = lax.rem((x * 8 + c * 4 + y), 2**m) * n
@@ -302,14 +302,18 @@
         kvr[(C2_A + i) * B : (C2_A + i + 1) * B] = halve(kvr, (C1_A + 2 * i) * B, B)
     cs3[0] = halve(kvr, C2_A * B, B)
     cs3[1, rows(64 * k, 64), :] = halve(kvr, 30 * B, 64)
+    levels = (cs3, cs4, cs5, cs6, cs7)
+
+    def send_levels(job):
+        for m in range(5):
+            if m:
+                levels[m][job] = halve(levels[m - 1].at[job], 0, B >> m)
+            send_subtrees(m, lambda job, at, n: levels[m].at[job], sib, sb_s, sb_r, jobs=(job,))
+
+    send_levels(0)
     cx.wait_recv()
     cs3[1, rows(64 * (1 - k), 64), :] = halve(c2o, 0, 64)
-    levels = (cs3, cs4, cs5, cs6, cs7)
-    for m in range(5):
-        if m:
-            for job in range(2):
-                levels[m][job] = halve(levels[m - 1].at[job], 0, B >> m)
-        send_subtrees(m, lambda job, at, n: levels[m].at[job], sib, sb_s, sb_r)
+    send_levels(1)
     send_own(qgs, qgr, qg_s, qg_r)
 
     def put_step(i, _):

time: 90.5 us -> 90.5 us (level)
  no operation moved by 1% of the time
where the time goes in v6:
time: 90.5 us; the launch traced here: 89.4 us
  Pallas kernels  88.8 us (98%)
    pallas_call x1, Pallas kernels, on_device(): pl.pallas_call(kernel, out_shape=[jax.ShapeDtypeStruct((12, n, B), F32) f...  86.3 us
    pallas_call x1, Pallas kernels, on_device(): pl.pallas_call(unpack, grid=(HEADS // 6,), out_shape=[jax.ShapeDtypeStruc...  2.52 us

profile of v6, /device:TPU:6, one launch (start us, length us, event | category | flops | bytes accessed | tf_op | source)
XLA Modules:
  0.0 89.4 jit_solution(3862374603846114824)
XLA Ops:
  0.6 86.3 %shard_map.75 = (f32[12,128,128]{2,1,0:T(8,128)}, f32[12,128,128]{2,1,0:T(8,128)}, f32[12,16,128]{2,1,0:T(8,128)}) custom-call(f32[128,768]{1,0:T(8,128)} %q_hbm.1, f32[128,768]{1,0:T(8,128)} %k_hbm.1, f32[128,768]{1,0:T(8,128)} %v_hbm.1, f32[128,768]{1,0:T(8,128)} %g_hbm.1), custom_call_target="tpu_custom_call" | custom-call | tf_op jit(solution)/shard_map/pallas_call | solution.py:562
  86.9 2.5 %shard_map.76 = (f32[128,768]{1,0:T(8,128)}, f32[128,768]{1,0:T(8,128)}, f32[128,768]{1,0:T(8,128)}, f32[128,768]{1,0:T(8,128)}) custom-call(f32[12,128,128]{2,1,0:T(8,128)} %get-tuple-element.7.qa, f32[12,128,128]{2,1,0:T(8,128)} %get-tuple-element.8.kv, f32[12,16,128]{2,1,0:T(8,128)} %get-tuple-element.9.c3), custom_call_target="tpu_custom_call" | custom-call | tf_op jit(solution)/shard_map/pallas_call | solution.py:572
